TPU v7x, 256 devices: a whole 4x4x8 slice. The times are simulated.
256 devices in a mesh: rep: 2 (over core), feat: 4 (over y), vert: 32 (over x, z).
Axes of the slice: x: 4, y: 4, z: 8, core: 2. Of those that a mesh axis runs over, the one named last changes fastest.
Arguments:
- features: bfloat16 [2, 32768, 768], P('rep', 'vert', 'feat'), may hold values from -6 to 6
- tile_ids: int32 [2, 256, 16], P('rep', 'vert'), may hold values from 0 to 255
- tile_count: int32 [2, 256], P('rep', 'vert'), may hold values from 1 to 16, as said below
- tiles: bfloat16 [2, 256, 16, 128, 128], P('rep', 'vert'), may hold values from -0.125 to 0.125
- self_weight: bfloat16 [768, 1024], P('feat'), may hold values from -0.21875 to 0.21875
- neigh_weight: bfloat16 [768, 1024], P('feat'), may hold values from -0.21875 to 0.21875
- bias: float32 [1024], replicated, may hold values from -3 to 3
- cotangent: bfloat16 [2, 32768, 1024], P('rep', 'vert', 'feat'), may hold values from -6 to 6
Outputs:
- hidden: bfloat16 [2, 32768, 1024], P('rep', 'vert', 'feat')
- feature_grad: bfloat16 [2, 32768, 768], P('rep', 'vert', 'feat')
- self_grad: float32 [768, 1024], P('feat')
- neigh_grad: float32 [768, 1024], P('feat')
Inputs may be any that keep to these rules, and one draw needn't show every extreme that they name: Only the first tile_count slots of a block row are used; in each batch some block row uses all 16 slots. `tile_ids`: column blocks are numbered within the batch.
All inputs are finite; a program needn't handle non-finite values.
Results may differ from a plain program's by a relative error of at most 0.018.
Values may be sent and summed in bfloat16 or wider, within the bound.
A program may use at most 128 MiB of HBM per device.

v0:
```python
import jax
import jax.numpy as jnp
from jax import lax
from jax.sharding import PartitionSpec as P


def silu_slope(value):
    sigmoid = jax.nn.sigmoid(value)
    return sigmoid * (1.0 + value * (1.0 - sigmoid))


def contract_rows(left, right):
    return lax.dot_general(
        left, right, (((0,), (0,)), ((), ())), preferred_element_type=jnp.float32
    )


def contract_cols(left, right):
    return lax.dot_general(
        left, right, (((1,), (1,)), ((), ())), preferred_element_type=jnp.float32
    )


def shards(features, tile_ids, tile_count, tiles, self_weight, neigh_weight, bias, cotangent):
    local_rows = features[0]
    width_here = local_rows.shape[1]
    edge = tiles.shape[-1]
    owned_blocks = tile_ids.shape[1]
    per_row = tile_ids.shape[2]
    hidden_here = cotangent.shape[2]
    every_row = lax.all_gather(local_rows, "vert", axis=0, tiled=True)
    block_table = every_row.reshape(-1, edge, width_here)
    total_blocks = block_table.shape[0]
    column_ids = tile_ids[0].reshape(-1)
    chosen = jnp.take(block_table, column_ids, axis=0).reshape(
        owned_blocks, per_row, edge, width_here
    )
    present = (jnp.arange(per_row, dtype=jnp.int32)[None, :] < tile_count[0][:, None]).astype(
        tiles.dtype
    )
    masked_tiles = tiles[0] * present[:, :, None, None]
    summed = jnp.einsum("bkij,bkjf->bif", masked_tiles, chosen, preferred_element_type=jnp.float32)
    neighbours = summed.astype(jnp.bfloat16).reshape(-1, width_here)
    partial_value = jnp.dot(local_rows, self_weight, preferred_element_type=jnp.float32) + jnp.dot(
        neighbours, neigh_weight, preferred_element_type=jnp.float32
    )
    offset = lax.axis_index("feat") * hidden_here
    preact = lax.psum_scatter(
        partial_value.astype(jnp.bfloat16), "feat", scatter_dimension=1, tiled=True
    ).astype(jnp.float32) + lax.dynamic_slice_in_dim(bias, offset, hidden_here)
    output_here = jax.nn.silu(preact).astype(jnp.bfloat16)
    slope_share = (cotangent[0].astype(jnp.float32) * silu_slope(preact)).astype(jnp.bfloat16)
    slope_full = lax.all_gather(slope_share, "feat", axis=1, tiled=True)
    self_term = contract_rows(local_rows, slope_full)
    neigh_term = contract_rows(neighbours, slope_full)
    self_grad, neigh_grad = lax.psum((self_term, neigh_term), ("rep", "vert"))
    back = contract_cols(slope_full, neigh_weight).astype(jnp.bfloat16)
    contrib = jnp.einsum(
        "bkij,bif->bkjf",
        masked_tiles,
        back.reshape(owned_blocks, edge, width_here),
        preferred_element_type=jnp.float32,
    )
    scattered = jax.ops.segment_sum(
        contrib.reshape(-1, edge, width_here), column_ids, num_segments=total_blocks
    )
    incoming = lax.psum_scatter(
        scattered.reshape(-1, width_here).astype(jnp.bfloat16),
        "vert",
        scatter_dimension=0,
        tiled=True,
    ).astype(jnp.float32)
    self_back = contract_cols(slope_full, self_weight)
    feature_grad = (self_back + incoming).astype(jnp.bfloat16)
    return (output_here[None], feature_grad[None], self_grad, neigh_grad)


def solution(mesh):
    return jax.shard_map(
        shards,
        mesh=mesh,
        in_specs=(
            P("rep", "vert", "feat"),
            P("rep", "vert", None),
            P("rep", "vert"),
            P("rep", "vert", None, None, None),
            P("feat", None),
            P("feat", None),
            P(),
            P("rep", "vert", "feat"),
        ),
        out_specs=(
            P("rep", "vert", "feat"),
            P("rep", "vert", "feat"),
            P("feat", None),
            P("feat", None),
        ),
        check_vma=False,
    )
```

profile of v0, /device:TPU:8, one launch (start us, length us, event | category | flops | bytes accessed | tf_op | source)
XLA Modules:
  0.0 760.3 jit_solution(3447526009804123918)
XLA Ops:
  7.2 0.0 copy-start
  7.2 0.0 all-gather.6.cloned.1.call-start
  7.2 0.7 all-gather.6.cloned.1.call-update
  7.9 0.0 reduce-scatter.3.cloned.1.call-start
  8.0 0.8 reshape_squeeze.6
  8.7 0.8 fusion.30
  9.5 3.9 fusion.26
  13.4 119.7 %all-gather.6.cloned.1.call-done = bf16[1,32768,192]{1,2,0:T(8,128)(2,1)} async-done(((bf16[1,1024,192]{1,2,0:T(8,128)(2,1)}), bf16[1,32768,192]{1,2,0:T(8,128)(2,1)}) %all-gather.6.cloned.1.call-update) | async-done | bytes 12582928 | tf_op jit(solution)/shard_map/all_gather | solution.py:31
  133.2 7.4 copy.28
  140.5 29.3 %copy.18 = bf16[256,128,192]{1,2,0:T(8,128)(2,1)} copy(bf16[256,128,192]{1,0,2:T(8,128)(2,1)S(1)} %bitcast.73) | data formatting | bytes 25165824 | tf_op jit(solution)/shard_map/reshape | solution.py:32
  169.9 8.5 %gather_fusion = bf16[128,128,192]{1,2,0:T(8,128)(2,1)} fusion(bf16[256,128,192]{1,2,0:T(8,128)(2,1)} %copy.18, s32[1024]{0:T(1024)S(1)} %pad_clamp_fusion), kind=kCustom, calls=%fused_computation | custom fusion | bytes 12583424 | tf_op jit(solution)/shard_map/jit(_take)/gather | solution.py:35
  178.4 0.0 copy-start.2
  178.4 6.1 fusion.16
  184.5 0.0 copy-done
  184.5 0.0 copy-done.2
  184.5 0.0 copy-start.6
  184.5 0.0 copy-start.8
  184.5 2.1 add_convert_fusion
  186.6 0.0 reduce-scatter.3.cloned.1.call-update
  186.6 0.0 all-gather.4.cloned.1.call-start
  186.7 0.8 dynamic_slice.3
  187.4 27.4 %reduce-scatter.3.cloned.1.call-done = bf16[1024,256]{1,0:T(8,128)(2,1)} async-done(((bf16[1024,1024]{1,0:T(8,128)(2,1)}), bf16[1024,256]{1,0:T(8,128)(2,1)}) %reduce-scatter.3.cloned.1.call-update) | async-done | bytes 524304 | tf_op jit(solution)/shard_map/reduce_scatter | solution.py:48
  214.9 0.0 copy-done.6
  214.9 2.5 fusion.19
  217.4 0.0 all-gather.4.cloned.1.call-update
  217.4 0.2 reduce-scatter.5.cloned.1.call-start
  217.6 0.0 copy-done.8
  217.6 0.1 reshape.103
  217.7 37.2 %all-gather.4.cloned.1.call-done = bf16[1024,1024]{1,0:T(8,128)(2,1)} async-done(((bf16[1024,256]{1,0:T(8,128)(2,1)}), bf16[1024,1024]{1,0:T(8,128)(2,1)}) %all-gather.4.cloned.1.call-update) | async-done | bytes 2097168 | tf_op jit(solution)/shard_map/all_gather | solution.py:53
  254.9 0.0 copy-start.3
  254.9 2.6 fusion.14
  257.5 0.1 copy.29
  257.6 0.2 copy-done.3
  257.7 6.5 fusion.3
  264.2 11.5 %broadcast_in_dim.25 = f32[256,128,192]{1,2,0:T(8,128)} broadcast(f32[]{:T(128)} %constant.31.clone.1), dimensions={} | broadcast | bytes 25165828 | tf_op jit(solution)/shard_map/broadcast_in_dim | solution.py:64
  275.7 32.8 %scatter_fusion = f32[256,128,192]{1,2,0:T(8,128)} fusion(f32[256,128,192]{1,2,0:T(8,128)} %broadcast_in_dim.25, s32[128]{0:T(128)S(1)} %reshape.103, f32[128,128,192]{1,2,0:T(8,128)} %bitcast.72), kind=kCustom, calls=%fused_computation.1 | custom fusion | flops 3145728 | bytes 37749248 | tf_op jit(solution)/shard_map/scatter-add | solution.py:64
  308.5 13.2 %copy_bitcast_fusion = bf16[32768,192]{0,1:T(8,128)(2,1)} fusion(f32[256,128,192]{1,2,0:T(8,128)} %scatter_fusion), kind=kLoop, calls=%fused_computation.2 | loop fusion | flops 6291456 | bytes 37748736 | tf_op jit(solution)/shard_map/convert_element_type | solution.py:68
  321.7 0.0 copy-start.4
  321.7 0.0 copy-start.5
  321.7 0.0 reduce-scatter.5.cloned.1.call-update
  321.7 0.0 copy-start.7
  321.7 0.0 all-reduce.3.cloned.1.call-start
  321.8 1.5 copy-done.4
  323.3 0.0 copy-done.5
  323.3 1.5 convolution_bitcast_fusion
  324.8 0.0 copy-start.1
  324.8 1.5 fusion.21
  326.2 0.0 all-reduce.3.cloned.1.call-update
  326.3 233.1 %reduce-scatter.5.cloned.1.call-done = bf16[1024,192]{0,1:T(8,128)(2,1)} async-done(((bf16[32768,192]{0,1:T(8,128)(2,1)}), bf16[1024,192]{0,1:T(8,128)(2,1)}) %reduce-scatter.5.cloned.1.call-update) | async-done | bytes 393232 | tf_op jit(solution)/shard_map/reduce_scatter | solution.py:67
  559.4 0.0 copy-done.7
  559.4 2.6 fusion.15
  562.0 187.6 %all-reduce.3.cloned.1.call-done = (f32[192,1024]{1,0:T(8,128)}, f32[192,1024]{1,0:T(8,128)}) async-done(((f32[192,1024]{1,0:T(8,128)}, f32[192,1024]{1,0:T(8,128)}), (f32[192,1024]{1,0:T(8,128)}, f32[192,1024]{1,0:T(8,128)})) %all-reduce.3.cloned.1.call-update) | async-done | bytes 1572880 | tf_op jit(solution)/shard_map/psum | solution.py:56
  749.6 2.1 copy.44
  751.7 2.1 copy.45
  753.8 0.0 copy-done.1
  (2 shorter events, 0.0 us)
Async XLA Ops:
  7.2 177.3 %copy-start = (bf16[192,1024]{1,0:T(8,128)(2,1)S(1)}, bf16[192,1024]{1,0:T(8,128)(2,1)}, u32[]{:S(2)}) copy-start(bf16[192,1024]{1,0:T(8,128)(2,1)} %param.13) | copy-start | bytes 1179652
  7.2 126.0 %all-gather.6.cloned.1.call-start = ((), (), s32[]{:S(2)}) async-start(), calls=%async_computation.5 | async-start | bytes 12976128 | tf_op jit(solution)/shard_map/all_gather | solution.py:31
  7.9 206.9 %reduce-scatter.3.cloned.1.call-start = ((), (), s32[]{:S(2)}) async-start(), calls=%async_computation.2 | async-start | bytes 2621440 | tf_op jit(solution)/shard_map/reduce_scatter | solution.py:48
  178.4 6.1 copy-start.2
  184.5 30.4 %copy-start.6 = (bf16[1,1024,256]{2,1,0:T(8,128)(2,1)S(1)}, bf16[1,1024,256]{2,1,0:T(8,128)(2,1)}, u32[]{:S(2)}) copy-start(bf16[1,1024,256]{2,1,0:T(8,128)(2,1)} %param.15) | copy-start | bytes 1572868
  184.5 33.1 %copy-start.8 = (s32[1,8,16]{2,1,0:T(8,128)S(1)}, s32[1,8,16]{2,1,0:T(8,128)}, u32[]{:S(2)}) copy-start(s32[1,8,16]{2,1,0:T(8,128)} %param.9) | copy-start | bytes 1540
  186.6 68.3 %all-gather.4.cloned.1.call-start = ((), (), s32[]{:S(2)}) async-start(), calls=%async_computation.3 | async-start | bytes 2621440 | tf_op jit(solution)/shard_map/all_gather | solution.py:53
  217.4 342.0 %reduce-scatter.5.cloned.1.call-start = ((), (), s32[]{:S(2)}) async-start(), calls=%async_computation.4 | async-start | bytes 12976128 | tf_op jit(solution)/shard_map/reduce_scatter | solution.py:67
  254.9 2.8 copy-start.3
  321.7 1.6 copy-start.4
  321.7 1.6 copy-start.5
  321.7 237.7 %copy-start.7 = (bf16[192,1024]{1,0:T(8,128)(2,1)S(1)}, bf16[192,1024]{1,0:T(8,128)(2,1)}, u32[]{:S(2)}) copy-start(bf16[192,1024]{1,0:T(8,128)(2,1)} %param.12) | copy-start | bytes 1179652
  321.7 427.9 %all-reduce.3.cloned.1.call-start = ((), (), s32[]{:S(2)}) async-start(), calls=%async_computation.6 | async-start | bytes 3145728 | tf_op jit(solution)/shard_map/psum | solution.py:56
  324.8 429.0 %copy-start.1 = (bf16[192,1024]{1,0:T(8,128)(2,1)S(1)}, bf16[192,1024]{1,0:T(8,128)(2,1)}, u32[]{:S(2)}) copy-start(bf16[192,1024]{1,0:T(8,128)(2,1)} %param.13) | copy-start | bytes 1179652
Sparse Core Ops, SparseCore 0:
  10.6 122.4 all-gather.5
  186.7 28.0 reduce-scatter.2
  217.5 37.3 all-gather.3
  321.8 237.5 reduce-scatter.4
  563.7 185.8 all-reduce.2
where the time goes:
time: 761 us; the launch traced here: 760 us
  waiting for transfers between devices  606 us (80%)
  local copies, waits for them, and re-layouts  64.3 us (8%)
  other arithmetic  49.3 us (6%)
  matrix products  26.6 us (3%)
  between operations  13.9 us (2%)
    reduce_scatter x1, waiting for transfers between devices, shards(): lax.psum_scatter(scattered.reshape(-1, width_here).astype(jnp.bfloat16),...  233 us
    psum x1, waiting for transfers between devices, shards(): self_grad, neigh_grad = lax.psum((self_term, neigh_term), ('rep', 'vert'))  188 us
    all_gather x1, waiting for transfers between devices, shards(): every_row = lax.all_gather(local_rows, 'vert', axis=0, tiled=True)  120 us
    all_gather x1, waiting for transfers between devices, shards(): slope_full = lax.all_gather(slope_share, 'feat', axis=1, tiled=True)  37.2 us
    scatter-add x1, other arithmetic, shards(): jax.ops.segment_sum(contrib.reshape(-1, edge, width_here), column_ids, nu...  32.8 us
    reshape x1, local copies, waits for them, and re-layouts, shards(): block_table = every_row.reshape(-1, edge, width_here)  29.3 us
    reduce_scatter x1, waiting for transfers between devices, shards(): lax.psum_scatter(partial_value.astype(jnp.bfloat16), 'feat', scatter_dime...  27.4 us
  transfers between devices with their start and end apart: 5, of which 5 were waited for; matrix products, arithmetic and copies ran while one was open for 2% of the time, Pallas kernels for 0%

commit v1 on v0

v1 whole, which is shorter than its diff:
```python
import functools
import heapq

import jax
import jax.numpy as jnp
from jax import lax
from jax.experimental import pallas as pl
from jax.experimental.pallas import tpu as pltpu
from jax.sharding import PartitionSpec as P

MESH = pl.DeviceIdType.MESH
F32 = jnp.float32
BF16 = jnp.bfloat16
RING_X = 4
RING_Z = 8
RING_Y = 4
FEAT_ROWS = 192
SHARD_COLS = 1024
HID_ROWS = 256
EDGE = 128
BLOCKS = RING_X * RING_Z * 8
CHUNKS = 4
CHUNK_COLS = SHARD_COLS // CHUNKS
SPLIT_A = 80


class Message:
    def __init__(self, axis, way, dx, dz, low, size, needs):
        self.axis, self.way, self.dx, self.dz = axis, way, dx, dz
        self.low, self.size, self.needs = low, size, needs


def half_rows(low, size, flip):
    first = (size // 32) * 16
    if flip:
        first = size - first
    return (low, first), (low + first, size - first)


def gather_messages(split):
    found = []

    def ring(axis, count, low, size, other, roots, flip):
        reached = {}
        last = count // 2
        parts = half_rows(low, size, flip)
        for way in (1, -1):
            before = list(roots)
            for step in range(1, last + 1):
                place = -way * step
                if step == last:
                    place = last
                    low_here, size_here = parts[0] if way == 1 else parts[1]
                else:
                    low_here, size_here = low, size
                dx, dz = (place, other) if axis == "x" else (other, place)
                found.append(Message(axis, way, dx, dz, low_here, size_here, list(before)))
                before = [len(found) - 1]
                reached.setdefault(place, []).append(len(found) - 1)
        return reached

    first_x = ring("x", RING_X, 0, split, 0, [], False)
    first_z = ring("z", RING_Z, split, FEAT_ROWS - split, 0, [], False)
    first_x[0] = []
    first_z[0] = []
    for turn, (place, roots) in enumerate(sorted(first_x.items(), key=lambda item: abs(item[0]))):
        ring("z", RING_Z, 0, split, place, roots, turn % 2 == 0)
    for turn, (place, roots) in enumerate(sorted(first_z.items(), key=lambda item: abs(item[0]))):
        ring("x", RING_X, split, FEAT_ROWS - split, place, roots, turn % 2 == 0)
    return found


def timed_order(found, needs, towards):
    count = len(found)
    followers = [[] for _ in range(count)]
    missing = [len(needs[i]) for i in range(count)]
    for i in range(count):
        for j in needs[i]:
            followers[j].append(i)
    depth = [0] * count

    def longest(i):
        if not depth[i]:
            depth[i] = found[i].size + max([longest(j) for j in followers[i]], default=0)
        return depth[i]

    for i in range(count):
        longest(i)
    waiting = {}
    busy = {}
    events = []
    steps = []
    tick = [0]

    def push(when, kind, what):
        tick[0] += 1
        heapq.heappush(events, (when, tick[0], kind, what))

    def offer(i, when):
        steps.append(("send", i))
        link = (found[i].axis, found[i].way * towards)
        start = max(when, busy.get(link, 0.0))
        busy[link] = start + found[i].size
        push(busy[link] + 30.0, "recv", i)

    for i in sorted((i for i in range(count) if missing[i] == 0), key=lambda i: -depth[i]):
        offer(i, 0.0)
    while events:
        when, _, kind, what = heapq.heappop(events)
        steps.append(("recv", what))
        ready = []
        for j in followers[what]:
            missing[j] -= 1
            if missing[j] == 0:
                ready.append(j)
        for j in sorted(ready, key=lambda j: -depth[j]):
            offer(j, when)
    return steps


def vert_of(x, z):
    return lax.rem(x + 2 * RING_X, RING_X) * RING_Z + lax.rem(z + 2 * RING_Z, RING_Z)


def dot_plain(left, right):
    return lax.dot_general(left, right, (((1,), (0,)), ((), ())), preferred_element_type=F32)


def dot_rows(left, right):
    return lax.dot_general(left, right, (((1,), (1,)), ((), ())), preferred_element_type=F32)


def unit(size):
    row = lax.broadcasted_iota(jnp.int32, (size, size), 0)
    col = lax.broadcasted_iota(jnp.int32, (size, size), 1)
    return jnp.where(row == col, 1.0, 0.0).astype(BF16)


class YRing:
    def __init__(self, send_sem, recv_sem, base, view, rows, me_y):
        self.send_sem, self.recv_sem, self.base = send_sem, recv_sem, base
        self.view, self.rows, self.me = view, rows, me_y

    def copy(self, number, owner, low, size, to):
        src = self.view(owner, low, size)
        return pltpu.make_async_remote_copy(
            src_ref=src, dst_ref=src,
            send_sem=self.send_sem.at[self.base + number],
            recv_sem=self.recv_sem.at[self.base + number],
            device_id={"feat": to}, device_id_type=MESH)

    def near(self, number):
        way = 1 if number == 0 else -1
        return self.copy(number, self.me, 0, self.rows, lax.rem(self.me + way + 4, 4))

    def far(self, number):
        way = 1 if number == 0 else -1
        half = self.rows // 2
        owner = lax.rem(self.me - way + 4, 4)
        return self.copy(2 + number, owner, number * half, half, lax.rem(self.me + way + 4, 4))

    def start(self):
        self.near(0).start()
        self.near(1).start()

    def hand_on(self):
        for number in (0, 1):
            self.near(number).wait_recv()
            self.far(number).start()

    def finish(self):
        for number in (0, 1):
            self.far(number).wait_recv()

    def drain(self):
        for number in (0, 1):
            self.near(number).wait_send()
            self.far(number).wait_send()


def forward_kernel(found, steps, feat_ref, ids_ref, tiles_hbm, ws_ref, wn_ref, bias_ref,
                   cot_ref, hidden_ref, slope_hbm, neigh_hbm,
                   table, tiles_v, feat_all, ws_all, wn_all, ws_t, wn_t, neigh_all, slope_all,
                   self_pre, cot_t,
                   send_sem, recv_sem, y_send, y_recv, w_send, w_recv, local_sem):
    vert = lax.axis_index("vert")
    me_y = lax.axis_index("feat")
    x, z = vert // RING_Z, lax.rem(vert, RING_Z)

    barrier = pltpu.get_barrier_semaphore()
    for step in (1, -1):
        pl.semaphore_signal(barrier, inc=1, device_id={"vert": vert_of(x + step, z)}, device_id_type=MESH)
        pl.semaphore_signal(barrier, inc=1, device_id={"vert": vert_of(x, z + step)}, device_id_type=MESH)
    for step in range(1, RING_Y):
        pl.semaphore_signal(barrier, inc=1, device_id={"feat": lax.rem(me_y + step, RING_Y)}, device_id_type=MESH)

    for part in range(8):
        table[vert * 8 + part] = feat_ref[:, part * EDGE:(part + 1) * EDGE]
    own_y = pltpu.make_async_copy(feat_ref, feat_all.at[me_y], local_sem.at[1])
    own_y.start()
    load_tiles = pltpu.make_async_copy(tiles_hbm, tiles_v, local_sem.at[2])
    load_tiles.start()
    own_y.wait()
    pl.semaphore_wait(barrier, 4 + RING_Y - 1)

    def message(i, sending):
        m = found[i]
        shift = m.way if sending else 0
        dx = m.dx + (shift if m.axis == "x" else 0)
        dz = m.dz + (shift if m.axis == "z" else 0)
        part = table.at[pl.ds(vert_of(x + dx, z + dz) * 8, 8), pl.ds(m.low, m.size), :]
        to = vert_of(x + m.way, z) if m.axis == "x" else vert_of(x, z + m.way)
        return pltpu.make_async_remote_copy(
            src_ref=part, dst_ref=part, send_sem=send_sem.at[i], recv_sem=recv_sem.at[i],
            device_id={"vert": to}, device_id_type=MESH)

    feat_ring = YRing(y_send, y_recv, 0, lambda o, low, size: feat_all.at[o, pl.ds(low, size), :],
                      FEAT_ROWS, me_y)

    def weight_copy(which, step):
        source, target = ((ws_ref, ws_all), (wn_ref, wn_all))[which]
        to = lax.rem(me_y + step, RING_Y)
        place = which * 3 + step - 1
        return pltpu.make_async_remote_copy(
            src_ref=source.at[:, pl.ds(pl.multiple_of(to * HID_ROWS, HID_ROWS), HID_ROWS)],
            dst_ref=target.at[me_y],
            send_sem=w_send.at[place], recv_sem=w_recv.at[place],
            device_id={"feat": to}, device_id_type=MESH)

    def weight_arrival(which, step):
        source, target = ((ws_ref, ws_all), (wn_ref, wn_all))[which]
        place = which * 3 + step - 1
        return pltpu.make_async_remote_copy(
            src_ref=source.at[:, pl.ds(0, HID_ROWS)],
            dst_ref=target.at[lax.rem(me_y - step + RING_Y, RING_Y)],
            send_sem=w_send.at[place], recv_sem=w_recv.at[place],
            device_id={"feat": lax.rem(me_y + step, RING_Y)}, device_id_type=MESH)

    def prepare_start():
        feat_ring.start()
        for which in (0, 1):
            for step in range(1, RING_Y):
                weight_copy(which, step).start()
        table[BLOCKS] = jnp.zeros((FEAT_ROWS, EDGE), BF16)
        mine = pl.ds(pl.multiple_of(me_y * HID_ROWS, HID_ROWS), HID_ROWS)
        ws_all[me_y] = ws_ref[:, mine]
        wn_all[me_y] = wn_ref[:, mine]
        for c in range(CHUNKS):
            span = pl.ds(c * CHUNK_COLS, CHUNK_COLS)
            cot_t[:, span] = dot_rows(unit(HID_ROWS), cot_ref[span, :]).astype(BF16)

    def prepare_weights():
        for which in (0, 1):
            for step in range(1, RING_Y):
                weight_arrival(which, step).wait_recv()
        for y in range(RING_Y):
            ws_t[y] = dot_rows(unit(HID_ROWS), ws_all[y]).astype(BF16)
            wn_t[y] = dot_rows(unit(HID_ROWS), wn_all[y]).astype(BF16)

    def prepare_self(c):
        span = pl.ds(c * CHUNK_COLS, CHUNK_COLS)
        total = jnp.concatenate([jnp.broadcast_to(bias_ref[...], (EDGE, HID_ROWS)).T] * (CHUNK_COLS // EDGE), axis=1)
        for y in range(RING_Y):
            total = total + dot_plain(ws_t[y], feat_all[y, :, span])
        self_pre[:, span] = total

    side = {8: prepare_start, 16: feat_ring.hand_on, 20: prepare_weights, 24: feat_ring.finish}
    for c in range(CHUNKS):
        side[30 + 6 * c] = functools.partial(prepare_self, c)

    arrived = 0
    for kind, i in steps:
        if kind == "send":
            message(i, True).start()
        else:
            message(i, False).wait_recv()
            arrived += 1
            if arrived in side:
                side[arrived]()
    load_tiles.wait()

    neigh_rings = [
        YRing(y_send, y_recv, 4 + 4 * c,
              lambda o, low, size, c=c: neigh_all.at[o, c, pl.ds(low, size), :], FEAT_ROWS, me_y)
        for c in range(CHUNKS)]
    slope_rings = [
        YRing(y_send, y_recv, 4 + 4 * CHUNKS + 4 * c,
              lambda o, low, size, c=c: slope_all.at[o, c, pl.ds(low, size), :], HID_ROWS, me_y)
        for c in range(CHUNKS)]

    def aggregate(b):
        total = jnp.zeros((FEAT_ROWS, EDGE), F32)
        for pair in range(8):
            left, right = [], []
            for k in (2 * pair, 2 * pair + 1):
                left.append(table[ids_ref[b * 16 + k]])
                right.append(tiles_v[b * 16 + k])
            total = total + dot_rows(jnp.concatenate(left, axis=1), jnp.concatenate(right, axis=1))
        return total.astype(BF16)

    per_chunk = CHUNK_COLS // EDGE
    for c in range(CHUNKS):
        for part in range(per_chunk):
            neigh_all[me_y, c, :, part * EDGE:(part + 1) * EDGE] = aggregate(c * per_chunk + part)
        neigh_rings[c].start()
        if c:
            neigh_rings[c - 1].hand_on()
    neigh_out = pltpu.make_async_copy(neigh_all.at[me_y], neigh_hbm, local_sem.at[3])
    neigh_out.start()
    neigh_rings[CHUNKS - 1].hand_on()

    for c in range(CHUNKS):
        span = pl.ds(c * CHUNK_COLS, CHUNK_COLS)
        neigh_rings[c].finish()
        value = self_pre[:, span]
        for y in range(RING_Y):
            value = value + dot_plain(wn_t[y], neigh_all[y, c])
        sigmoid = jax.nn.sigmoid(value)
        slope = cot_t[:, span].astype(F32) * (sigmoid * (1.0 + value * (1.0 - sigmoid)))
        slope_all[me_y, c] = slope.astype(BF16)
        slope_rings[c].start()
        if c:
            slope_rings[c - 1].hand_on()
        hidden_t = (value * sigmoid).astype(BF16)
        for part in range(per_chunk):
            hidden_ref[pl.ds(c * CHUNK_COLS + part * EDGE, EDGE), :] = dot_rows(
                unit(EDGE), hidden_t[:, part * EDGE:(part + 1) * EDGE]).astype(BF16)
    slope_rings[CHUNKS - 1].hand_on()
    for c in range(CHUNKS):
        slope_rings[c].finish()
    slope_out = pltpu.make_async_copy(slope_all, slope_hbm, local_sem.at[4])
    slope_out.start()

    for i in range(len(found)):
        message(i, True).wait_send()
    feat_ring.drain()
    for which in (0, 1):
        for step in range(1, RING_Y):
            weight_copy(which, step).wait_send()
    for ring in neigh_rings + slope_rings:
        ring.drain()
    neigh_out.wait()
    slope_out.wait()


def backward_kernel(found, steps, offsets, wants, feat_ref, order_ref, row_ref, same_ref, last_ref, tiles_hbm,
                    ws_ref, wn_ref, slope_ref, neigh_ref,
                    grad_ref, self_ref, neigh_grad_ref,
                    tiles_v, back_v, seg, table, landed, grad_v, sums, total_v,
                    first_in, second_in, third_in, third_v, final_v,
                    send_sem, recv_sem, w_send, w_recv, local_sem):
    vert = lax.axis_index("vert")
    rep = lax.axis_index("rep")
    x, z = vert // RING_Z, lax.rem(vert, RING_Z)

    barrier = pltpu.get_barrier_semaphore()
    for step in range(1, RING_X):
        pl.semaphore_signal(barrier, inc=1, device_id={"vert": vert_of(x + step, z)}, device_id_type=MESH)
    for step in range(1, RING_Z):
        pl.semaphore_signal(barrier, inc=1, device_id={"vert": vert_of(x, z + step)}, device_id_type=MESH)
    pl.semaphore_signal(barrier, inc=1, device_id={"rep": 1 - rep}, device_id_type=MESH)

    load_tiles = pltpu.make_async_copy(tiles_hbm, tiles_v, local_sem.at[0])
    load_tiles.start()
    per_chunk = CHUNK_COLS // EDGE
    for c in range(CHUNKS):
        value = jnp.zeros((FEAT_ROWS, CHUNK_COLS), F32)
        for y in range(RING_Y):
            value = value + dot_plain(wn_ref[:, y * HID_ROWS:(y + 1) * HID_ROWS], slope_ref[y, c])
        value = value.astype(BF16)
        for part in range(per_chunk):
            back_v[c * per_chunk + part] = value[:, part * EDGE:(part + 1) * EDGE]
    load_tiles.wait()

    seg[128] = jnp.zeros((FEAT_ROWS, EDGE), BF16)

    def spread(turn, carry):
        for inner in range(8):
            p = turn * 8 + inner
            slot = order_ref[p]
            part = dot_plain(back_v[row_ref[p]], tiles_v[slot])
            keep = same_ref[p].astype(F32)
            value = part + total_v[:, 0:EDGE] * keep
            total_v[:, 0:EDGE] = value
            seg[p] = value.astype(BF16)
        return carry

    total_v[:, 0:EDGE] = jnp.zeros((FEAT_ROWS, EDGE), F32)
    lax.fori_loop(0, 16, spread, 0)

    def fill(owner, carry):
        for part in range(8):
            table[owner * 8 + part] = seg[last_ref[owner * 8 + part]]
        return carry

    lax.fori_loop(0, RING_X * RING_Z, fill, 0)
    pl.semaphore_wait(barrier, RING_X - 1 + RING_Z - 1 + 1)

    def message(i):
        m = found[i]
        to = vert_of(x - m.way, z) if m.axis == "x" else vert_of(x, z - m.way)
        return pltpu.make_async_remote_copy(
            src_ref=table.at[pl.ds(vert_of(x + m.dx, z + m.dz) * 8, 8), pl.ds(m.low, m.size), :],
            dst_ref=landed.at[:, pl.ds(offsets[i], m.size), :],
            send_sem=send_sem.at[i], recv_sem=recv_sem.at[i],
            device_id={"vert": to}, device_id_type=MESH)

    def absorb(i):
        m = found[i]
        dx = m.dx + (m.way if m.axis == "x" else 0)
        dz = m.dz + (m.way if m.axis == "z" else 0)
        mine = not m.needs
        owner = vert_of(x + dx, z + dz)

        def rows(step, carry):
            here = pl.ds(pl.multiple_of(offsets[i] + step * 16, 16), 16)
            there = pl.ds(pl.multiple_of(m.low + step * 16, 16), 16)
            for part in range(8):
                value = landed[part, here, :].astype(F32)
                if mine:
                    span = slice(part * EDGE, (part + 1) * EDGE)
                    total_v[there, span] = total_v[there, span] + value
                else:
                    place = owner * 8 + part
                    table[place, there, :] = (table[place, there, :].astype(F32) + value).astype(BF16)
            return carry

        lax.fori_loop(0, m.size // 16, rows, 0)

    def copy_to(source, target, number, axis, step):
        if axis == "rep":
            device = {"rep": 1 - rep}
        else:
            device = {"vert": vert_of(x + step, z) if axis == "x" else vert_of(x, z + step)}
        return pltpu.make_async_remote_copy(
            src_ref=source, dst_ref=target, send_sem=w_send.at[number], recv_sem=w_recv.at[number],
            device_id=device, device_id_type=MESH)

    def swap_rep():
        return copy_to(grad_v.at[1 - rep], first_in, 0, "rep", 0)

    def scatter_x(step):
        to = lax.rem(x + step, RING_X)
        return copy_to(sums.at[pl.ds(pl.multiple_of(to * 48, 48), 48), :], second_in.at[step - 1], step, "x", step)

    def scatter_z(step):
        to = lax.rem(z + step, RING_Z)
        return copy_to(third_v.at[to], third_in.at[step - 1], 3 + step, "z", step)

    def gather_z(step):
        mine = final_v.at[rep, x, z]
        return copy_to(mine, mine, 10 + step, "z", step)

    def gather_x(step):
        mine = final_v.at[rep, x]
        return copy_to(mine, mine, 17 + step, "x", step)

    def share_rep():
        return copy_to(final_v.at[rep], final_v.at[rep], 21, "rep", 0)

    def landing(target, number, axis):
        return copy_to(target, target, number, axis, 1)

    def weight_sums():
        for y in range(RING_Y):
            span = slice(y * HID_ROWS, (y + 1) * HID_ROWS)
            one = jnp.zeros((FEAT_ROWS, HID_ROWS), F32)
            two = jnp.zeros((FEAT_ROWS, HID_ROWS), F32)
            for c in range(CHUNKS):
                piece = slope_ref[y, c]
                one = one + dot_rows(feat_ref[:, c * CHUNK_COLS:(c + 1) * CHUNK_COLS], piece)
                two = two + dot_rows(neigh_ref[c], piece)
            grad_v[0, :, span] = one
            grad_v[1, :, span] = two
        swap_rep().start()

    def own_total():
        for c in range(CHUNKS):
            span = slice(c * CHUNK_COLS, (c + 1) * CHUNK_COLS)
            value = jnp.concatenate(
                [table[vert * 8 + c * per_chunk + part] for part in range(per_chunk)], axis=1).astype(F32)
            for y in range(RING_Y):
                value = value + dot_plain(ws_ref[:, y * HID_ROWS:(y + 1) * HID_ROWS], slope_ref[y, c])
            total_v[:, span] = value

    def after_rep():
        landing(first_in, 0, "rep").wait_recv()
        sums[...] = grad_v[rep] + first_in[...]
        for step in range(1, RING_X):
            scatter_x(step).start()

    def after_x():
        for step in range(1, RING_X):
            landing(second_in.at[step - 1], step, "x").wait_recv()
        mine = sums[pl.ds(pl.multiple_of(x * 48, 48), 48), :] + second_in[0] + second_in[1] + second_in[2]
        for part in range(RING_Z):
            third_v[part] = mine[:, part * EDGE:(part + 1) * EDGE]
        for step in range(1, RING_Z):
            scatter_z(step).start()

    def after_z():
        for step in range(1, RING_Z):
            landing(third_in.at[step - 1], 3 + step, "z").wait_recv()
        value = third_v[z]
        for step in range(1, RING_Z):
            value = value + third_in[step - 1]
        final_v[rep, x, z] = value
        for step in range(1, RING_Z):
            gather_z(step).start()

    def gathered_z():
        for step in range(1, RING_Z):
            landing(final_v.at[rep, x, lax.rem(z - step + RING_Z, RING_Z)], 10 + step, "z").wait_recv()
        for step in range(1, RING_X):
            gather_x(step).start()

    def gathered_x():
        for step in range(1, RING_X):
            landing(final_v.at[rep, lax.rem(x - step + RING_X, RING_X)], 17 + step, "x").wait_recv()
        share_rep().start()

    side = {0: lambda: (weight_sums(), own_total()), 6: after_rep, 16: after_x, 26: after_z,
            36: gathered_z, 46: gathered_x}
    arrived = 0
    for kind, i in steps:
        if kind == "recv":
            if arrived in side:
                side[arrived]()
            message(i).wait_recv()
            absorb(i)
            arrived += 1
        else:
            message(i).start()

    grad_ref[...] = total_v[...].astype(BF16)
    landing(final_v.at[1 - rep], 21, "rep").wait_recv()
    for number, target in ((0, self_ref), (1, neigh_grad_ref)):
        for row in range(RING_X):
            for part in range(RING_Z):
                target[row * 48:(row + 1) * 48, part * EDGE:(part + 1) * EDGE] = final_v[number, row, part]

    for i in range(len(found)):
        message(i).wait_send()
    swap_rep().wait_send()
    for step in range(1, RING_X):
        scatter_x(step).wait_send()
        gather_x(step).wait_send()
    for step in range(1, RING_Z):
        scatter_z(step).wait_send()
        gather_z(step).wait_send()
    share_rep().wait_send()


def live_keys(ids, counts):
    live = jnp.arange(16, dtype=jnp.int32)[None, :] < counts[:, None]
    return jnp.where(live, ids, BLOCKS).reshape(-1)


def sort_slots(key):
    slot = jnp.arange(128, dtype=jnp.int32)
    full = key * 128 + slot
    rank = jnp.sum((full[None, :] < full[:, None]).astype(jnp.int32), axis=1)
    hit = rank[None, :] == slot[:, None]
    order = jnp.sum(jnp.where(hit, slot[None, :], 0), axis=1)
    before = rank[None, :] == slot[:, None] - 1
    sorted_key = jnp.sum(jnp.where(hit, key[None, :], 0), axis=1)
    prior_key = jnp.sum(jnp.where(before, key[None, :] + 1, 0), axis=1) - 1
    same = (sorted_key == prior_key).astype(jnp.int32)
    block = jnp.arange(256, dtype=jnp.int32)
    upto = jnp.sum((key[None, :] <= block[:, None]).astype(jnp.int32), axis=1)
    any_here = jnp.any(key[None, :] == block[:, None], axis=1)
    last = jnp.where(any_here, upto - 1, 128)
    return order, order // 16, same, last


def shards(features, tile_ids, tile_count, tiles, self_weight, neigh_weight, bias, cotangent):
    feat_t = features[0].T
    key = live_keys(tile_ids[0], tile_count[0])
    flat_tiles = tiles[0].reshape(128, EDGE, EDGE)
    bias_here = lax.dynamic_slice_in_dim(bias, lax.axis_index("feat") * HID_ROWS, HID_ROWS)[None, :]

    found = gather_messages(SPLIT_A)
    needs = [m.needs for m in found]
    steps = timed_order(found, needs, 1)
    vmem = pl.BlockSpec(memory_space=pltpu.VMEM)
    smem = pl.BlockSpec(memory_space=pltpu.SMEM)
    anywhere = pl.BlockSpec(memory_space=pl.ANY)
    dma = pltpu.SemaphoreType.DMA
    rings = 4 + 8 * CHUNKS
    hidden, slope_all, neigh = pl.pallas_call(
        functools.partial(forward_kernel, found, steps),
        name="gather_aggregate",
        out_shape=(
            jax.ShapeDtypeStruct((SHARD_COLS, HID_ROWS), BF16),
            jax.ShapeDtypeStruct((RING_Y, CHUNKS, HID_ROWS, CHUNK_COLS), BF16),
            jax.ShapeDtypeStruct((CHUNKS, FEAT_ROWS, CHUNK_COLS), BF16),
        ),
        in_specs=[vmem, smem, anywhere, vmem, vmem, vmem, vmem],
        out_specs=(vmem, anywhere, anywhere),
        scratch_shapes=[
            pltpu.VMEM((BLOCKS + 1, FEAT_ROWS, EDGE), BF16),
            pltpu.VMEM((128, EDGE, EDGE), BF16),
            pltpu.VMEM((RING_Y, FEAT_ROWS, SHARD_COLS), BF16),
            pltpu.VMEM((RING_Y, FEAT_ROWS, HID_ROWS), BF16),
            pltpu.VMEM((RING_Y, FEAT_ROWS, HID_ROWS), BF16),
            pltpu.VMEM((RING_Y, HID_ROWS, FEAT_ROWS), BF16),
            pltpu.VMEM((RING_Y, HID_ROWS, FEAT_ROWS), BF16),
            pltpu.VMEM((RING_Y, CHUNKS, FEAT_ROWS, CHUNK_COLS), BF16),
            pltpu.VMEM((RING_Y, CHUNKS, HID_ROWS, CHUNK_COLS), BF16),
            pltpu.VMEM((HID_ROWS, SHARD_COLS), F32),
            pltpu.VMEM((HID_ROWS, SHARD_COLS), BF16),
            dma((len(found),)), dma((len(found),)),
            dma((rings,)), dma((rings,)),
            dma((6,)), dma((6,)),
            dma((5,)),
        ],
        compiler_params=pltpu.CompilerParams(
            collective_id=0, has_side_effects=True, vmem_limit_bytes=48 * 1024 * 1024),
        cost_estimate=pl.CostEstimate(flops=3 * 10**9, bytes_accessed=10**7, transcendentals=262144),
    )(feat_t, key, flat_tiles, self_weight, neigh_weight, bias_here, cotangent[0])

    order, row, same, last = sort_slots(key)
    wants = [[j for j in range(len(found)) if i in found[j].needs] for i in range(len(found))]
    back_steps = timed_order(found, wants, -1)
    offsets, at = [], 0
    for m in found:
        offsets.append(at)
        at += m.size
    grad_t, self_grad, neigh_grad = pl.pallas_call(
        functools.partial(backward_kernel, found, back_steps, offsets, wants),
        name="spread_reduce",
        out_shape=(
            jax.ShapeDtypeStruct((FEAT_ROWS, SHARD_COLS), BF16),
            jax.ShapeDtypeStruct((FEAT_ROWS, SHARD_COLS), F32),
            jax.ShapeDtypeStruct((FEAT_ROWS, SHARD_COLS), F32),
        ),
        in_specs=[vmem, smem, smem, smem, smem, anywhere, vmem, vmem, vmem, vmem],
        out_specs=(vmem, vmem, vmem),
        scratch_shapes=[
            pltpu.VMEM((128, EDGE, EDGE), BF16),
            pltpu.VMEM((8, FEAT_ROWS, EDGE), BF16),
            pltpu.VMEM((129, FEAT_ROWS, EDGE), BF16),
            pltpu.VMEM((BLOCKS, FEAT_ROWS, EDGE), BF16),
            pltpu.VMEM((8, at, EDGE), BF16),
            pltpu.VMEM((2, FEAT_ROWS, SHARD_COLS), F32),
            pltpu.VMEM((FEAT_ROWS, SHARD_COLS), F32),
            pltpu.VMEM((FEAT_ROWS, SHARD_COLS), F32),
            pltpu.VMEM((FEAT_ROWS, SHARD_COLS), F32),
            pltpu.VMEM((3, 48, SHARD_COLS), F32),
            pltpu.VMEM((7, 48, EDGE), F32),
            pltpu.VMEM((8, 48, EDGE), F32),
            pltpu.VMEM((2, RING_X, RING_Z, 48, EDGE), F32),
            dma((len(found),)), dma((len(found),)),
            dma((22,)), dma((22,)),
            dma((1,)),
        ],
        compiler_params=pltpu.CompilerParams(
            collective_id=1, has_side_effects=True, vmem_limit_bytes=56 * 1024 * 1024),
        cost_estimate=pl.CostEstimate(flops=3 * 10**9, bytes_accessed=10**7, transcendentals=0),
    )(feat_t, order, row, same, last, flat_tiles, self_weight, neigh_weight, slope_all, neigh)
    return (hidden[None], grad_t.T[None], self_grad, neigh_grad)


def solution(mesh):
    return jax.shard_map(
        shards,
        mesh=mesh,
        in_specs=(
            P("rep", "vert", "feat"),
            P("rep", "vert", None),
            P("rep", "vert"),
            P("rep", "vert", None, None, None),
            P("feat", None),
            P("feat", None),
            P(),
            P("rep", "vert", "feat"),
        ),
        out_specs=(
            P("rep", "vert", "feat"),
            P("rep", "vert", "feat"),
            P("feat", None),
            P("feat", None),
        ),
        check_vma=False,
    )
```

time: 761 us -> 238 us (0.31)
  waiting for transfers between devices: 606 us -> 0 us
  Pallas kernels: 0 us -> 219 us
  local copies, waits for them, and re-layouts: 64.3 us -> 14.5 us
  other arithmetic: 49.3 us -> 3.03 us
  matrix products: 26.6 us -> 0 us
  between operations: 13.9 us -> 0.7 us
    reduce_scatter x2 -> x0, waiting for transfers between devices: 261 us -> none  [the longest x1 233 us: shards(): lax.psum_scatter(scattered.reshape(-1, width_here).astype(jnp.bfloat16),...]
    pallas_call x0 -> x2, Pallas kernels: none -> 219 us  [the longest x1 113 us: shards(): pl.pallas_call(functools.partial(forward_kernel, found, steps), name='gat...]
    psum x1 -> x0, waiting for transfers between devices: 188 us -> none  [shards(): self_grad, neigh_grad = lax.psum((self_term, neigh_term), ('rep', 'vert'))]
    all_gather x2 -> x0, waiting for transfers between devices: 157 us -> none  [the longest x1 120 us: shards(): every_row = lax.all_gather(local_rows, 'vert', axis=0, tiled=True)]
    scatter-add x1 -> x0, other arithmetic: 32.8 us -> none  [shards(): jax.ops.segment_sum(contrib.reshape(-1, edge, width_here), column_ids, nu...]
    reshape x1 -> x0, local copies, waits for them, and re-layouts: 29.3 us -> none  [shards(): block_table = every_row.reshape(-1, edge, width_here)]
    dot_general x8 -> x0, matrix products: 26.6 us -> none  [the longest x1 6.45 us: shards(): jnp.einsum('bkij,bif->bkjf', masked_tiles, back.reshape(owned_blocks, edg...]
    convert_element_type x3 -> x1, other arithmetic: 16.5 us -> 0.58 us  [sort_slots(): same = (sorted_key == prior_key).astype(jnp.int32)]
  transfers between devices with their start and end apart: 5 -> 0, of which waited for: 5 -> 0; matrix products, arithmetic and copies ran while one was open for 2% -> 0% of each run, Pallas kernels for 0% -> 0%
where the time goes in v1:
time: 238 us
  Pallas kernels  219 us (92%)
  local copies, waits for them, and re-layouts  14.5 us (6%)
  other arithmetic  3.03 us (1%)
    pallas_call x1, Pallas kernels, shards(): pl.pallas_call(functools.partial(forward_kernel, found, steps), name='gat...  113 us
    pallas_call x1, Pallas kernels, shards(): pl.pallas_call(functools.partial(backward_kernel, found, back_steps, offs...  107 us
    unnamed x18, local copies, waits for them, and re-layouts  12.9 us

profile of v1, /device:TPU:8, one launch (start us, length us, event | category | flops | bytes accessed | tf_op | source)
XLA Modules:
  0.0 237.7 jit_solution(7465453362805060881)
XLA Ops:
  0.6 0.8 squeeze.10
  1.4 0.8 dynamic_slice.3
  2.2 0.7 iota_compare_fusion.3
  2.9 0.1 lt.54
  3.0 0.2 convert_reduce_fusion.1
  3.2 0.1 fusion
  3.3 0.2 select_reduce_fusion
  3.5 0.0 copy-start.6
  3.5 0.6 compare_convert_fusion.same_ref
  4.1 0.5 and_select_fusion.row_ref
  4.6 0.1 convert_reduce_fusion
  4.7 0.6 add_select_fusion.last_ref
  5.3 0.0 copy-start
  5.3 1.0 copy-done
  6.4 0.0 copy-start.1
  6.4 1.0 copy-done.1
  7.4 0.0 copy-start.2
  7.4 1.0 copy-done.2
  8.3 0.0 copy-start.3
  8.4 1.0 copy-done.3
  9.3 112.6 %gather_aggregate.1 = (bf16[1024,256]{1,0:T(8,128)(2,1)S(1)}, bf16[4,4,256,256]{3,2,1,0:T(8,128)(2,1)S(1)}, bf16[4,192,256]{2,1,0:T(8,128)(2,1)S(1)}) custom-call(bf16[192,1024]{1,0:T(8,128)(2,1)S(1)} %bitcast.15, s32[128]{0:T(128)S(1)} %get-tuple-element.20.ids_ref, bf16[128,128,128]{2,1,0:T(8,128)(2,1)} %bitcast.17, bf16[192,1024]{1,0:T(8,128)(2,1)S(1)} %copy-done.2, ...), custom_call_target="tpu_custom_call" | custom-call | flops 3000000000 | bytes 10000000 | tf_op jit(solution)/shard_map/gather_aggregate/pallas_call | solution.py:590
  122.0 0.0 copy-done.6
  122.0 0.0 copy-start.4
  122.0 1.3 copy-done.4
  123.3 0.0 copy-start.5
  123.3 0.7 copy-done.5
  124.1 106.9 %spread_reduce.1 = (bf16[192,1024]{1,0:T(8,128)(2,1)}, f32[192,1024]{1,0:T(8,128)}, f32[192,1024]{1,0:T(8,128)}) custom-call(bf16[192,1024]{1,0:T(8,128)(2,1)} %bitcast.14, s32[128]{0:T(128)} %copy-done.6, s32[128]{0:T(128)} %and_select_fusion.row_ref, s32[128]{0:T(128)} %compare_convert_fusion.same_ref, s32[256]{0:T(256)} %add_select_fusion.last_ref, ...), custom_call_target="tpu_custom_call" | custom-call | flops 3000000000 | bytes 10000000 | tf_op jit(solution)/shard_map/spread_reduce/pallas_call | solution.py:629
  230.9 0.8 copy.16
  231.7 1.8 copy.17
  233.5 2.1 copy.18
  235.6 2.1 copy.19
  (2 shorter events, 0.0 us)
Async XLA Ops:
  3.5 118.4 %copy-start.6 = (s32[128]{0:T(128)}, s32[128]{0:T(128)S(1)}, u32[]{:S(2)}) copy-start(s32[128]{0:T(128)S(1)} %get-tuple-element.18.order_ref) | copy-start | bytes 1540
  5.3 1.0 copy-start
  6.4 1.0 copy-start.1
  7.4 1.0 copy-start.2
  8.3 1.0 copy-start.3
  122.0 1.4 copy-start.4
  123.3 0.7 copy-start.5

commit v2 on v1

--- a/solution.py
+++ b/solution.py
@@ -178,32 +178,47 @@
             self.far(number).wait_send()
 
 
-def forward_kernel(found, steps, feat_ref, ids_ref, tiles_hbm, ws_ref, wn_ref, bias_ref,
-                   cot_ref, hidden_ref, slope_hbm, neigh_hbm,
-                   table, tiles_v, feat_all, ws_all, wn_all, ws_t, wn_t, neigh_all, slope_all,
-                   self_pre, cot_t,
-                   send_sem, recv_sem, y_send, y_recv, w_send, w_recv, local_sem):
+def layer_kernel(found, steps, back_steps, offsets, feat_hbm, ids_ref, order_ref, row_ref, same_ref, last_ref,
+                 tiles_hbm, ws_hbm, wn_hbm, bias_ref, cot_hbm,
+                 hidden_hbm, grad_hbm, self_hbm, neigh_hbm,
+                 table, tiles_v, ws_v, wn_v, cot_v, hidden_v, feat_all, ws_all, wn_all, ws_t, wn_t,
+                 neigh_all, slope_all, self_pre, cot_t,
+                 back_v, seg, landed, grad_v, sums, total_v, grad_v16,
+                 first_in, second_in, third_in, third_v, final_v,
+                 ag_send, ag_recv, rs_send, rs_recv, y_send, y_recv, w_send, w_recv, ar_send, ar_recv, local_sem):
     vert = lax.axis_index("vert")
+    rep = lax.axis_index("rep")
     me_y = lax.axis_index("feat")
     x, z = vert // RING_Z, lax.rem(vert, RING_Z)
 
     barrier = pltpu.get_barrier_semaphore()
-    for step in (1, -1):
+    for step in range(1, RING_X):
         pl.semaphore_signal(barrier, inc=1, device_id={"vert": vert_of(x + step, z)}, device_id_type=MESH)
+    for step in range(1, RING_Z):
         pl.semaphore_signal(barrier, inc=1, device_id={"vert": vert_of(x, z + step)}, device_id_type=MESH)
+    pl.semaphore_signal(barrier, inc=1, device_id={"rep": 1 - rep}, device_id_type=MESH)
     for step in range(1, RING_Y):
         pl.semaphore_signal(barrier, inc=1, device_id={"feat": lax.rem(me_y + step, RING_Y)}, device_id_type=MESH)
 
-    for part in range(8):
-        table[vert * 8 + part] = feat_ref[:, part * EDGE:(part + 1) * EDGE]
-    own_y = pltpu.make_async_copy(feat_ref, feat_all.at[me_y], local_sem.at[1])
-    own_y.start()
-    load_tiles = pltpu.make_async_copy(tiles_hbm, tiles_v, local_sem.at[2])
-    load_tiles.start()
-    own_y.wait()
-    pl.semaphore_wait(barrier, 4 + RING_Y - 1)
-
-    def message(i, sending):
+    mine_h = pl.ds(pl.multiple_of(me_y * HID_ROWS, HID_ROWS), HID_ROWS)
+    own = [pltpu.make_async_copy(feat_hbm.at[:, pl.ds(part * EDGE, EDGE)], table.at[vert * 8 + part],
+                                 local_sem.at[part]) for part in range(8)]
+    inputs = [
+        pltpu.make_async_copy(feat_hbm, feat_all.at[me_y], local_sem.at[8]),
+        pltpu.make_async_copy(ws_hbm, ws_v, local_sem.at[9]),
+        pltpu.make_async_copy(wn_hbm, wn_v, local_sem.at[10]),
+        pltpu.make_async_copy(ws_hbm.at[:, mine_h], ws_all.at[me_y], local_sem.at[11]),
+        pltpu.make_async_copy(wn_hbm.at[:, mine_h], wn_all.at[me_y], local_sem.at[12]),
+        pltpu.make_async_copy(cot_hbm, cot_v, local_sem.at[13]),
+        pltpu.make_async_copy(tiles_hbm, tiles_v, local_sem.at[14]),
+    ]
+    for copy in own + inputs:
+        copy.start()
+    for copy in own:
+        copy.wait()
+    pl.semaphore_wait(barrier, RING_X - 1 + RING_Z - 1 + 1 + RING_Y - 1)
+
+    def forward_message(i, sending):
         m = found[i]
         shift = m.way if sending else 0
         dx = m.dx + (shift if m.axis == "x" else 0)
@@ -211,14 +226,14 @@
         part = table.at[pl.ds(vert_of(x + dx, z + dz) * 8, 8), pl.ds(m.low, m.size), :]
         to = vert_of(x + m.way, z) if m.axis == "x" else vert_of(x, z + m.way)
         return pltpu.make_async_remote_copy(
-            src_ref=part, dst_ref=part, send_sem=send_sem.at[i], recv_sem=recv_sem.at[i],
+            src_ref=part, dst_ref=part, send_sem=ag_send.at[i], recv_sem=ag_recv.at[i],
             device_id={"vert": to}, device_id_type=MESH)
 
     feat_ring = YRing(y_send, y_recv, 0, lambda o, low, size: feat_all.at[o, pl.ds(low, size), :],
                       FEAT_ROWS, me_y)
 
     def weight_copy(which, step):
-        source, target = ((ws_ref, ws_all), (wn_ref, wn_all))[which]
+        source, target = ((ws_v, ws_all), (wn_v, wn_all))[which]
         to = lax.rem(me_y + step, RING_Y)
         place = which * 3 + step - 1
         return pltpu.make_async_remote_copy(
@@ -228,7 +243,7 @@
             device_id={"feat": to}, device_id_type=MESH)
 
     def weight_arrival(which, step):
-        source, target = ((ws_ref, ws_all), (wn_ref, wn_all))[which]
+        source, target = ((ws_v, ws_all), (wn_v, wn_all))[which]
         place = which * 3 + step - 1
         return pltpu.make_async_remote_copy(
             src_ref=source.at[:, pl.ds(0, HID_ROWS)],
@@ -237,17 +252,16 @@
             device_id={"feat": lax.rem(me_y + step, RING_Y)}, device_id_type=MESH)
 
     def prepare_start():
+        for copy in inputs:
+            copy.wait()
         feat_ring.start()
         for which in (0, 1):
             for step in range(1, RING_Y):
                 weight_copy(which, step).start()
         table[BLOCKS] = jnp.zeros((FEAT_ROWS, EDGE), BF16)
-        mine = pl.ds(pl.multiple_of(me_y * HID_ROWS, HID_ROWS), HID_ROWS)
-        ws_all[me_y] = ws_ref[:, mine]
-        wn_all[me_y] = wn_ref[:, mine]
         for c in range(CHUNKS):
             span = pl.ds(c * CHUNK_COLS, CHUNK_COLS)
-            cot_t[:, span] = dot_rows(unit(HID_ROWS), cot_ref[span, :]).astype(BF16)
+            cot_t[:, span] = dot_rows(unit(HID_ROWS), cot_v[span, :]).astype(BF16)
 
     def prepare_weights():
         for which in (0, 1):
@@ -271,13 +285,12 @@
     arrived = 0
     for kind, i in steps:
         if kind == "send":
-            message(i, True).start()
+            forward_message(i, True).start()
         else:
-            message(i, False).wait_recv()
+            forward_message(i, False).wait_recv()
             arrived += 1
             if arrived in side:
                 side[arrived]()
-    load_tiles.wait()
 
     neigh_rings = [
         YRing(y_send, y_recv, 4 + 4 * c,
@@ -305,8 +318,6 @@
         neigh_rings[c].start()
         if c:
             neigh_rings[c - 1].hand_on()
-    neigh_out = pltpu.make_async_copy(neigh_all.at[me_y], neigh_hbm, local_sem.at[3])
-    neigh_out.start()
     neigh_rings[CHUNKS - 1].hand_on()
 
     for c in range(CHUNKS):
@@ -323,54 +334,21 @@
             slope_rings[c - 1].hand_on()
         hidden_t = (value * sigmoid).astype(BF16)
         for part in range(per_chunk):
-            hidden_ref[pl.ds(c * CHUNK_COLS + part * EDGE, EDGE), :] = dot_rows(
+            hidden_v[pl.ds(c * CHUNK_COLS + part * EDGE, EDGE), :] = dot_rows(
                 unit(EDGE), hidden_t[:, part * EDGE:(part + 1) * EDGE]).astype(BF16)
     slope_rings[CHUNKS - 1].hand_on()
+    hidden_out = pltpu.make_async_copy(hidden_v, hidden_hbm, local_sem.at[15])
+    hidden_out.start()
     for c in range(CHUNKS):
         slope_rings[c].finish()
-    slope_out = pltpu.make_async_copy(slope_all, slope_hbm, local_sem.at[4])
-    slope_out.start()
-
-    for i in range(len(found)):
-        message(i, True).wait_send()
-    feat_ring.drain()
-    for which in (0, 1):
-        for step in range(1, RING_Y):
-            weight_copy(which, step).wait_send()
-    for ring in neigh_rings + slope_rings:
-        ring.drain()
-    neigh_out.wait()
-    slope_out.wait()
-
-
-def backward_kernel(found, steps, offsets, wants, feat_ref, order_ref, row_ref, same_ref, last_ref, tiles_hbm,
-                    ws_ref, wn_ref, slope_ref, neigh_ref,
-                    grad_ref, self_ref, neigh_grad_ref,
-                    tiles_v, back_v, seg, table, landed, grad_v, sums, total_v,
-                    first_in, second_in, third_in, third_v, final_v,
-                    send_sem, recv_sem, w_send, w_recv, local_sem):
-    vert = lax.axis_index("vert")
-    rep = lax.axis_index("rep")
-    x, z = vert // RING_Z, lax.rem(vert, RING_Z)
-
-    barrier = pltpu.get_barrier_semaphore()
-    for step in range(1, RING_X):
-        pl.semaphore_signal(barrier, inc=1, device_id={"vert": vert_of(x + step, z)}, device_id_type=MESH)
-    for step in range(1, RING_Z):
-        pl.semaphore_signal(barrier, inc=1, device_id={"vert": vert_of(x, z + step)}, device_id_type=MESH)
-    pl.semaphore_signal(barrier, inc=1, device_id={"rep": 1 - rep}, device_id_type=MESH)
-
-    load_tiles = pltpu.make_async_copy(tiles_hbm, tiles_v, local_sem.at[0])
-    load_tiles.start()
-    per_chunk = CHUNK_COLS // EDGE
-    for c in range(CHUNKS):
         value = jnp.zeros((FEAT_ROWS, CHUNK_COLS), F32)
         for y in range(RING_Y):
-            value = value + dot_plain(wn_ref[:, y * HID_ROWS:(y + 1) * HID_ROWS], slope_ref[y, c])
+            value = value + dot_plain(wn_v[:, y * HID_ROWS:(y + 1) * HID_ROWS], slope_all[y, c])
         value = value.astype(BF16)
         for part in range(per_chunk):
             back_v[c * per_chunk + part] = value[:, part * EDGE:(part + 1) * EDGE]
-    load_tiles.wait()
+    for i in range(len(found)):
+        forward_message(i, True).wait_send()
 
     seg[128] = jnp.zeros((FEAT_ROWS, EDGE), BF16)
 
@@ -394,7 +372,6 @@
         return carry
 
     lax.fori_loop(0, RING_X * RING_Z, fill, 0)
-    pl.semaphore_wait(barrier, RING_X - 1 + RING_Z - 1 + 1)
 
     def message(i):
         m = found[i]
@@ -402,7 +379,7 @@
         return pltpu.make_async_remote_copy(
             src_ref=table.at[pl.ds(vert_of(x + m.dx, z + m.dz) * 8, 8), pl.ds(m.low, m.size), :],
             dst_ref=landed.at[:, pl.ds(offsets[i], m.size), :],
-            send_sem=send_sem.at[i], recv_sem=recv_sem.at[i],
+            send_sem=rs_send.at[i], recv_sem=rs_recv.at[i],
             device_id={"vert": to}, device_id_type=MESH)
 
     def absorb(i):
@@ -433,8 +410,14 @@
         else:
             device = {"vert": vert_of(x + step, z) if axis == "x" else vert_of(x, z + step)}
         return pltpu.make_async_remote_copy(
-            src_ref=source, dst_ref=target, send_sem=w_send.at[number], recv_sem=w_recv.at[number],
+            src_ref=source, dst_ref=target, send_sem=ar_send.at[number], recv_sem=ar_recv.at[number],
             device_id=device, device_id_type=MESH)
+
+    def final_rows(place):
+        return pl.ds(pl.multiple_of(place * 48, 48), 48)
+
+    def final_lanes(place):
+        return pl.ds(pl.multiple_of(place * EDGE, EDGE), EDGE)
 
     def swap_rep():
         return copy_to(grad_v.at[1 - rep], first_in, 0, "rep", 0)
@@ -448,11 +431,11 @@
         return copy_to(third_v.at[to], third_in.at[step - 1], 3 + step, "z", step)
 
     def gather_z(step):
-        mine = final_v.at[rep, x, z]
+        mine = final_v.at[rep, final_rows(x), final_lanes(z)]
         return copy_to(mine, mine, 10 + step, "z", step)
 
     def gather_x(step):
-        mine = final_v.at[rep, x]
+        mine = final_v.at[rep, final_rows(x), :]
         return copy_to(mine, mine, 17 + step, "x", step)
 
     def share_rep():
@@ -467,9 +450,9 @@
             one = jnp.zeros((FEAT_ROWS, HID_ROWS), F32)
             two = jnp.zeros((FEAT_ROWS, HID_ROWS), F32)
             for c in range(CHUNKS):
-                piece = slope_ref[y, c]
-                one = one + dot_rows(feat_ref[:, c * CHUNK_COLS:(c + 1) * CHUNK_COLS], piece)
-                two = two + dot_rows(neigh_ref[c], piece)
+                piece = slope_all[y, c]
+                one = one + dot_rows(feat_all[me_y, :, c * CHUNK_COLS:(c + 1) * CHUNK_COLS], piece)
+                two = two + dot_rows(neigh_all[me_y, c], piece)
             grad_v[0, :, span] = one
             grad_v[1, :, span] = two
         swap_rep().start()
@@ -480,7 +463,7 @@
             value = jnp.concatenate(
                 [table[vert * 8 + c * per_chunk + part] for part in range(per_chunk)], axis=1).astype(F32)
             for y in range(RING_Y):
-                value = value + dot_plain(ws_ref[:, y * HID_ROWS:(y + 1) * HID_ROWS], slope_ref[y, c])
+                value = value + dot_plain(ws_v[:, y * HID_ROWS:(y + 1) * HID_ROWS], slope_all[y, c])
             total_v[:, span] = value
 
     def after_rep():
@@ -504,25 +487,25 @@
         value = third_v[z]
         for step in range(1, RING_Z):
             value = value + third_in[step - 1]
-        final_v[rep, x, z] = value
+        final_v[rep, final_rows(x), final_lanes(z)] = value
         for step in range(1, RING_Z):
             gather_z(step).start()
 
     def gathered_z():
         for step in range(1, RING_Z):
-            landing(final_v.at[rep, x, lax.rem(z - step + RING_Z, RING_Z)], 10 + step, "z").wait_recv()
+            landing(final_v.at[rep, final_rows(x), final_lanes(lax.rem(z - step + RING_Z, RING_Z))], 10 + step, "z").wait_recv()
         for step in range(1, RING_X):
             gather_x(step).start()
 
     def gathered_x():
         for step in range(1, RING_X):
-            landing(final_v.at[rep, lax.rem(x - step + RING_X, RING_X)], 17 + step, "x").wait_recv()
+            landing(final_v.at[rep, final_rows(lax.rem(x - step + RING_X, RING_X)), :], 17 + step, "x").wait_recv()
         share_rep().start()
 
     side = {0: lambda: (weight_sums(), own_total()), 6: after_rep, 16: after_x, 26: after_z,
             36: gathered_z, 46: gathered_x}
     arrived = 0
-    for kind, i in steps:
+    for kind, i in back_steps:
         if kind == "recv":
             if arrived in side:
                 side[arrived]()
@@ -532,13 +515,14 @@
         else:
             message(i).start()
 
-    grad_ref[...] = total_v[...].astype(BF16)
     landing(final_v.at[1 - rep], 21, "rep").wait_recv()
-    for number, target in ((0, self_ref), (1, neigh_grad_ref)):
-        for row in range(RING_X):
-            for part in range(RING_Z):
-                target[row * 48:(row + 1) * 48, part * EDGE:(part + 1) * EDGE] = final_v[number, row, part]
-
+    outputs = [pltpu.make_async_copy(final_v.at[0], self_hbm, local_sem.at[17]),
+               pltpu.make_async_copy(final_v.at[1], neigh_hbm, local_sem.at[18])]
+    for copy in outputs:
+        copy.start()
+    grad_v16[...] = total_v[...].astype(BF16)
+    outputs.append(pltpu.make_async_copy(grad_v16, grad_hbm, local_sem.at[16]))
+    outputs[-1].start()
     for i in range(len(found)):
         message(i).wait_send()
     swap_rep().wait_send()
@@ -549,6 +533,24 @@
         scatter_z(step).wait_send()
         gather_z(step).wait_send()
     share_rep().wait_send()
+    feat_ring.drain()
+    for which in (0, 1):
+        for step in range(1, RING_Y):
+            weight_copy(which, step).wait_send()
+    for ring in neigh_rings + slope_rings:
+        ring.drain()
+    hidden_out.wait()
+    for copy in outputs:
+        copy.wait()
+
+
+def finish_kernel(*refs):
+    count = (len(refs) - 1) // 2
+    copies = [pltpu.make_async_copy(refs[i], refs[count + i], refs[-1].at[i]) for i in range(count)]
+    for copy in copies:
+        copy.start()
+    for copy in copies:
+        copy.wait()
 
 
 def live_keys(ids, counts):
@@ -579,27 +581,40 @@
     flat_tiles = tiles[0].reshape(128, EDGE, EDGE)
     bias_here = lax.dynamic_slice_in_dim(bias, lax.axis_index("feat") * HID_ROWS, HID_ROWS)[None, :]
 
+    order, row, same, last = sort_slots(key)
     found = gather_messages(SPLIT_A)
     needs = [m.needs for m in found]
     steps = timed_order(found, needs, 1)
+    wants = [[j for j in range(len(found)) if i in found[j].needs] for i in range(len(found))]
+    back_steps = timed_order(found, wants, -1)
+    offsets, at = [], 0
+    for m in found:
+        offsets.append(at)
+        at += m.size
     vmem = pl.BlockSpec(memory_space=pltpu.VMEM)
     smem = pl.BlockSpec(memory_space=pltpu.SMEM)
     anywhere = pl.BlockSpec(memory_space=pl.ANY)
     dma = pltpu.SemaphoreType.DMA
     rings = 4 + 8 * CHUNKS
-    hidden, slope_all, neigh = pl.pallas_call(
-        functools.partial(forward_kernel, found, steps),
-        name="gather_aggregate",
-        out_shape=(
-            jax.ShapeDtypeStruct((SHARD_COLS, HID_ROWS), BF16),
-            jax.ShapeDtypeStruct((RING_Y, CHUNKS, HID_ROWS, CHUNK_COLS), BF16),
-            jax.ShapeDtypeStruct((CHUNKS, FEAT_ROWS, CHUNK_COLS), BF16),
-        ),
-        in_specs=[vmem, smem, anywhere, vmem, vmem, vmem, vmem],
-        out_specs=(vmem, anywhere, anywhere),
+    results = (
+        jax.ShapeDtypeStruct((SHARD_COLS, HID_ROWS), BF16),
+        jax.ShapeDtypeStruct((FEAT_ROWS, SHARD_COLS), BF16),
+        jax.ShapeDtypeStruct((FEAT_ROWS, SHARD_COLS), F32),
+        jax.ShapeDtypeStruct((FEAT_ROWS, SHARD_COLS), F32),
+    )
+    held = pl.pallas_call(
+        functools.partial(layer_kernel, found, steps, back_steps, offsets),
+        name="layer",
+        out_shape=results,
+        in_specs=[anywhere, smem, smem, smem, smem, smem, anywhere, anywhere, anywhere, vmem, anywhere],
+        out_specs=(anywhere,) * 4,
         scratch_shapes=[
             pltpu.VMEM((BLOCKS + 1, FEAT_ROWS, EDGE), BF16),
             pltpu.VMEM((128, EDGE, EDGE), BF16),
+            pltpu.VMEM((FEAT_ROWS, SHARD_COLS), BF16),
+            pltpu.VMEM((FEAT_ROWS, SHARD_COLS), BF16),
+            pltpu.VMEM((SHARD_COLS, HID_ROWS), BF16),
+            pltpu.VMEM((SHARD_COLS, HID_ROWS), BF16),
             pltpu.VMEM((RING_Y, FEAT_ROWS, SHARD_COLS), BF16),
             pltpu.VMEM((RING_Y, FEAT_ROWS, HID_ROWS), BF16),
             pltpu.VMEM((RING_Y, FEAT_ROWS, HID_ROWS), BF16),
@@ -609,55 +624,37 @@
             pltpu.VMEM((RING_Y, CHUNKS, HID_ROWS, CHUNK_COLS), BF16),
             pltpu.VMEM((HID_ROWS, SHARD_COLS), F32),
             pltpu.VMEM((HID_ROWS, SHARD_COLS), BF16),
-            dma((len(found),)), dma((len(found),)),
-            dma((rings,)), dma((rings,)),
-            dma((6,)), dma((6,)),
-            dma((5,)),
-        ],
-        compiler_params=pltpu.CompilerParams(
-            collective_id=0, has_side_effects=True, vmem_limit_bytes=48 * 1024 * 1024),
-        cost_estimate=pl.CostEstimate(flops=3 * 10**9, bytes_accessed=10**7, transcendentals=262144),
-    )(feat_t, key, flat_tiles, self_weight, neigh_weight, bias_here, cotangent[0])
-
-    order, row, same, last = sort_slots(key)
-    wants = [[j for j in range(len(found)) if i in found[j].needs] for i in range(len(found))]
-    back_steps = timed_order(found, wants, -1)
-    offsets, at = [], 0
-    for m in found:
-        offsets.append(at)
-        at += m.size
-    grad_t, self_grad, neigh_grad = pl.pallas_call(
-        functools.partial(backward_kernel, found, back_steps, offsets, wants),
-        name="spread_reduce",
-        out_shape=(
-            jax.ShapeDtypeStruct((FEAT_ROWS, SHARD_COLS), BF16),
-            jax.ShapeDtypeStruct((FEAT_ROWS, SHARD_COLS), F32),
-            jax.ShapeDtypeStruct((FEAT_ROWS, SHARD_COLS), F32),
-        ),
-        in_specs=[vmem, smem, smem, smem, smem, anywhere, vmem, vmem, vmem, vmem],
-        out_specs=(vmem, vmem, vmem),
-        scratch_shapes=[
-            pltpu.VMEM((128, EDGE, EDGE), BF16),
             pltpu.VMEM((8, FEAT_ROWS, EDGE), BF16),
             pltpu.VMEM((129, FEAT_ROWS, EDGE), BF16),
-            pltpu.VMEM((BLOCKS, FEAT_ROWS, EDGE), BF16),
             pltpu.VMEM((8, at, EDGE), BF16),
             pltpu.VMEM((2, FEAT_ROWS, SHARD_COLS), F32),
             pltpu.VMEM((FEAT_ROWS, SHARD_COLS), F32),
             pltpu.VMEM((FEAT_ROWS, SHARD_COLS), F32),
+            pltpu.VMEM((FEAT_ROWS, SHARD_COLS), BF16),
             pltpu.VMEM((FEAT_ROWS, SHARD_COLS), F32),
             pltpu.VMEM((3, 48, SHARD_COLS), F32),
             pltpu.VMEM((7, 48, EDGE), F32),
             pltpu.VMEM((8, 48, EDGE), F32),
-            pltpu.VMEM((2, RING_X, RING_Z, 48, EDGE), F32),
+            pltpu.VMEM((2, FEAT_ROWS, SHARD_COLS), F32),
             dma((len(found),)), dma((len(found),)),
+            dma((len(found),)), dma((len(found),)),
+            dma((rings,)), dma((rings,)),
+            dma((6,)), dma((6,)),
             dma((22,)), dma((22,)),
-            dma((1,)),
+            dma((19,)),
         ],
         compiler_params=pltpu.CompilerParams(
-            collective_id=1, has_side_effects=True, vmem_limit_bytes=56 * 1024 * 1024),
-        cost_estimate=pl.CostEstimate(flops=3 * 10**9, bytes_accessed=10**7, transcendentals=0),
-    )(feat_t, order, row, same, last, flat_tiles, self_weight, neigh_weight, slope_all, neigh)
+            collective_id=0, has_side_effects=True, vmem_limit_bytes=58 * 1024 * 1024),
+        cost_estimate=pl.CostEstimate(flops=6 * 10**9, bytes_accessed=2 * 10**7, transcendentals=262144),
+    )(feat_t, key, order, row, same, last, flat_tiles, self_weight, neigh_weight, bias_here, cotangent[0])
+    hidden, grad_t, self_grad, neigh_grad = pl.pallas_call(
+        finish_kernel,
+        name="finish",
+        out_shape=results,
+        in_specs=[anywhere] * 4,
+        out_specs=(anywhere,) * 4,
+        scratch_shapes=[dma((4,))],
+    )(*held)
     return (hidden[None], grad_t.T[None], self_grad, neigh_grad)
 
 

time: 238 us -> 299 us (1.26)
  Pallas kernels: 219 us -> 293 us
  local copies, waits for them, and re-layouts: 14.5 us -> 2.19 us
    pallas_call x2, Pallas kernels: 219 us -> 293 us  [the longest x1 216 us: shards(): pl.pallas_call(functools.partial(layer_kernel, found, steps, back_steps,...]
    unnamed x18 -> x4, local copies, waits for them, and re-layouts: 12.9 us -> 0.01 us
where the time goes in v2:
time: 299 us
  Pallas kernels  293 us (98%)
  other arithmetic  3.1 us (1%)
    pallas_call x1, Pallas kernels, shards(): pl.pallas_call(functools.partial(layer_kernel, found, steps, back_steps,...  216 us
    pallas_call x1, Pallas kernels, shards(): pl.pallas_call(finish_kernel, name='finish', out_shape=results, in_specs=...  76.6 us

profile of v2, /device:TPU:8, one launch (start us, length us, event | category | flops | bytes accessed | tf_op | source)
XLA Modules:
  0.0 298.9 jit_solution(14425773447122592215)
XLA Ops:
  0.6 0.8 squeeze.10
  1.4 1.3 dynamic_slice.3
  2.7 0.7 iota_compare_fusion.3
  3.5 0.1 lt.54
  3.6 0.0 copy-start
  3.6 0.2 convert_reduce_fusion.1
  3.7 0.1 fusion
  3.9 0.2 select_reduce_fusion
  4.1 0.0 copy-start.1
  4.1 0.6 compare_convert_fusion.same_ref
  4.7 0.6 and_select_fusion.row_ref
  5.3 0.1 convert_reduce_fusion
  5.4 0.6 add_select_fusion.last_ref
  5.9 0.0 copy-done
  5.9 0.0 copy-done.1
  6.0 216.3 %layer.1 = (bf16[1024,256]{1,0:T(8,128)(2,1)}, bf16[192,1024]{1,0:T(8,128)(2,1)}, f32[192,1024]{1,0:T(8,128)}, f32[192,1024]{1,0:T(8,128)}) custom-call(bf16[192,1024]{1,0:T(8,128)(2,1)} %bitcast.15, s32[128]{0:T(128)} %copy-done, s32[128]{0:T(128)} %copy-done.1, s32[128]{0:T(128)} %and_select_fusion.row_ref, s32[128]{0:T(128)} %compare_convert_fusion.same_ref, ...), custom_call_target="tpu_custom_call" | custom-call | flops 6000000000 | bytes 20000000 | tf_op jit(solution)/shard_map/layer/pallas_call | solution.py:605
  222.3 76.6 %finish.1 = (bf16[1024,256]{1,0:T(8,128)(2,1)}, bf16[192,1024]{1,0:T(8,128)(2,1)}, f32[192,1024]{1,0:T(8,128)}, f32[192,1024]{1,0:T(8,128)}) custom-call(bf16[1024,256]{1,0:T(8,128)(2,1)} %get-tuple-element.12.refs_0_, bf16[192,1024]{1,0:T(8,128)(2,1)} %get-tuple-element.13.refs_1_, f32[192,1024]{1,0:T(8,128)} %get-tuple-element.14.refs_2_, ...), custom_call_target="tpu_custom_call" | custom-call | tf_op jit(solution)/shard_map/finish/pallas_call | solution.py:650
  (2 shorter events, 0.0 us)
Async XLA Ops:
  3.6 2.4 copy-start
  4.1 1.9 copy-start.1

commit v3 on v2

--- a/solution.py
+++ b/solution.py
@@ -178,13 +178,13 @@
             self.far(number).wait_send()
 
 
-def layer_kernel(found, steps, back_steps, offsets, feat_hbm, ids_ref, order_ref, row_ref, same_ref, last_ref,
+def layer_kernel(found, steps, back_steps, offsets, feat_hbm, ids_ref, count_ref,
                  tiles_hbm, ws_hbm, wn_hbm, bias_ref, cot_hbm,
-                 hidden_hbm, grad_hbm, self_hbm, neigh_hbm,
+                 hidden_hbm, grad_hbm, sums_hbm,
                  table, tiles_v, ws_v, wn_v, cot_v, hidden_v, feat_all, ws_all, wn_all, ws_t, wn_t,
                  neigh_all, slope_all, self_pre, cot_t,
                  back_v, seg, landed, grad_v, sums, total_v, grad_v16,
-                 first_in, second_in, third_in, third_v, final_v,
+                 half_v, half_sums, first_in, second_in, third_in, third_v, third_half, final_v, plan_v, plan,
                  ag_send, ag_recv, rs_send, rs_recv, y_send, y_recv, w_send, w_recv, ar_send, ar_recv, local_sem):
     vert = lax.axis_index("vert")
     rep = lax.axis_index("rep")
@@ -263,6 +263,43 @@
             span = pl.ds(c * CHUNK_COLS, CHUNK_COLS)
             cot_t[:, span] = dot_rows(unit(HID_ROWS), cot_v[span, :]).astype(BF16)
 
+    plan_copy = pltpu.make_async_copy(plan_v, plan, local_sem.at[17])
+
+    def prepare_plan():
+        lane = lax.broadcasted_iota(jnp.int32, (1, EDGE), 1)
+        named = jnp.zeros((1, EDGE), jnp.int32)
+        limit = jnp.zeros((1, EDGE), jnp.int32)
+        for b in range(8):
+            limit = jnp.where((lane >= b * 16) & (lane < b * 16 + 16), count_ref[b], limit)
+            for k in range(16):
+                named = jnp.where(lane == b * 16 + k, ids_ref[b, k], named)
+        key = jnp.where(lane - (lane >> 4) * 16 < limit, named, BLOCKS)
+        across = jnp.broadcast_to(key, (EDGE, EDGE))
+        down = across.T
+        row = lax.broadcasted_iota(jnp.int32, (EDGE, EDGE), 0)
+        col = lax.broadcasted_iota(jnp.int32, (EDGE, EDGE), 1)
+        ahead = (across * EDGE + col < down * EDGE + row).astype(jnp.int32)
+        rank = jnp.sum(ahead, axis=1, keepdims=True)
+        hit = rank == col
+
+        def pick(mask, value):
+            return jnp.sum(jnp.where(mask, value, 0), axis=0, keepdims=True)
+
+        order = pick(hit, row)
+        now = pick(hit, down)
+        prior = pick(rank == col - 1, down + 1) - 1
+        plan_v[0:1, :] = key
+        plan_v[1:2, :] = order
+        plan_v[2:3, :] = order >> 4
+        plan_v[3:4, :] = (now == prior).astype(jnp.int32)
+        for half in range(2):
+            block = col + half * EDGE
+            upto = pick(down <= block, 1)
+            here = pick(down == block, 1)
+            plan_v[4 + half:5 + half, :] = jnp.where(here > 0, upto - 1, 128)
+        plan_v[6:8, :] = jnp.zeros((2, EDGE), jnp.int32)
+        plan_copy.start()
+
     def prepare_weights():
         for which in (0, 1):
             for step in range(1, RING_Y):
@@ -273,12 +310,12 @@
 
     def prepare_self(c):
         span = pl.ds(c * CHUNK_COLS, CHUNK_COLS)
-        total = jnp.concatenate([jnp.broadcast_to(bias_ref[...], (EDGE, HID_ROWS)).T] * (CHUNK_COLS // EDGE), axis=1)
+        total = jnp.concatenate([jnp.broadcast_to(bias_ref[:, mine_h], (EDGE, HID_ROWS)).T] * (CHUNK_COLS // EDGE), axis=1)
         for y in range(RING_Y):
             total = total + dot_plain(ws_t[y], feat_all[y, :, span])
         self_pre[:, span] = total
 
-    side = {8: prepare_start, 16: feat_ring.hand_on, 20: prepare_weights, 24: feat_ring.finish}
+    side = {4: prepare_plan, 8: prepare_start, 12: plan_copy.wait, 16: feat_ring.hand_on, 20: prepare_weights, 24: feat_ring.finish}
     for c in range(CHUNKS):
         side[30 + 6 * c] = functools.partial(prepare_self, c)
 
@@ -306,7 +343,7 @@
         for pair in range(8):
             left, right = [], []
             for k in (2 * pair, 2 * pair + 1):
-                left.append(table[ids_ref[b * 16 + k]])
+                left.append(table[plan[0, b * 16 + k]])
                 right.append(tiles_v[b * 16 + k])
             total = total + dot_rows(jnp.concatenate(left, axis=1), jnp.concatenate(right, axis=1))
         return total.astype(BF16)
@@ -355,9 +392,9 @@
     def spread(turn, carry):
         for inner in range(8):
             p = turn * 8 + inner
-            slot = order_ref[p]
-            part = dot_plain(back_v[row_ref[p]], tiles_v[slot])
-            keep = same_ref[p].astype(F32)
+            slot = plan[1, p]
+            part = dot_plain(back_v[plan[2, p]], tiles_v[slot])
+            keep = plan[3, p].astype(F32)
             value = part + total_v[:, 0:EDGE] * keep
             total_v[:, 0:EDGE] = value
             seg[p] = value.astype(BF16)
@@ -368,7 +405,7 @@
 
     def fill(owner, carry):
         for part in range(8):
-            table[owner * 8 + part] = seg[last_ref[owner * 8 + part]]
+            table[owner * 8 + part] = seg[plan[4 + owner // 16, lax.rem(owner, 16) * 8 + part]]
         return carry
 
     lax.fori_loop(0, RING_X * RING_Z, fill, 0)
@@ -420,15 +457,15 @@
         return pl.ds(pl.multiple_of(place * EDGE, EDGE), EDGE)
 
     def swap_rep():
-        return copy_to(grad_v.at[1 - rep], first_in, 0, "rep", 0)
+        return copy_to(half_v.at[1 - rep], first_in, 0, "rep", 0)
 
     def scatter_x(step):
         to = lax.rem(x + step, RING_X)
-        return copy_to(sums.at[pl.ds(pl.multiple_of(to * 48, 48), 48), :], second_in.at[step - 1], step, "x", step)
+        return copy_to(half_sums.at[pl.ds(pl.multiple_of(to * 48, 48), 48), :], second_in.at[step - 1], step, "x", step)
 
     def scatter_z(step):
         to = lax.rem(z + step, RING_Z)
-        return copy_to(third_v.at[to], third_in.at[step - 1], 3 + step, "z", step)
+        return copy_to(third_half.at[to], third_in.at[step - 1], 3 + step, "z", step)
 
     def gather_z(step):
         mine = final_v.at[rep, final_rows(x), final_lanes(z)]
@@ -455,6 +492,8 @@
                 two = two + dot_rows(neigh_all[me_y, c], piece)
             grad_v[0, :, span] = one
             grad_v[1, :, span] = two
+            half_v[0, :, span] = one.astype(BF16)
+            half_v[1, :, span] = two.astype(BF16)
         swap_rep().start()
 
     def own_total():
@@ -468,16 +507,20 @@
 
     def after_rep():
         landing(first_in, 0, "rep").wait_recv()
-        sums[...] = grad_v[rep] + first_in[...]
+        sums[...] = grad_v[rep] + first_in[...].astype(F32)
+        half_sums[...] = sums[...].astype(BF16)
         for step in range(1, RING_X):
             scatter_x(step).start()
 
     def after_x():
         for step in range(1, RING_X):
             landing(second_in.at[step - 1], step, "x").wait_recv()
-        mine = sums[pl.ds(pl.multiple_of(x * 48, 48), 48), :] + second_in[0] + second_in[1] + second_in[2]
+        mine = sums[pl.ds(pl.multiple_of(x * 48, 48), 48), :]
+        for step in range(1, RING_X):
+            mine = mine + second_in[step - 1].astype(F32)
         for part in range(RING_Z):
             third_v[part] = mine[:, part * EDGE:(part + 1) * EDGE]
+            third_half[part] = mine[:, part * EDGE:(part + 1) * EDGE].astype(BF16)
         for step in range(1, RING_Z):
             scatter_z(step).start()
 
@@ -486,8 +529,8 @@
             landing(third_in.at[step - 1], 3 + step, "z").wait_recv()
         value = third_v[z]
         for step in range(1, RING_Z):
-            value = value + third_in[step - 1]
-        final_v[rep, final_rows(x), final_lanes(z)] = value
+            value = value + third_in[step - 1].astype(F32)
+        final_v[rep, final_rows(x), final_lanes(z)] = value.astype(BF16)
         for step in range(1, RING_Z):
             gather_z(step).start()
 
@@ -502,8 +545,8 @@
             landing(final_v.at[rep, final_rows(lax.rem(x - step + RING_X, RING_X)), :], 17 + step, "x").wait_recv()
         share_rep().start()
 
-    side = {0: lambda: (weight_sums(), own_total()), 6: after_rep, 16: after_x, 26: after_z,
-            36: gathered_z, 46: gathered_x}
+    side = {0: lambda: (weight_sums(), own_total()), 4: after_rep, 18: after_x, 32: after_z,
+            46: gathered_z, 60: gathered_x}
     arrived = 0
     for kind, i in back_steps:
         if kind == "recv":
@@ -516,8 +559,7 @@
             message(i).start()
 
     landing(final_v.at[1 - rep], 21, "rep").wait_recv()
-    outputs = [pltpu.make_async_copy(final_v.at[0], self_hbm, local_sem.at[17]),
-               pltpu.make_async_copy(final_v.at[1], neigh_hbm, local_sem.at[18])]
+    outputs = [pltpu.make_async_copy(final_v, sums_hbm, local_sem.at[18])]
     for copy in outputs:
         copy.start()
     grad_v16[...] = total_v[...].astype(BF16)
@@ -544,44 +586,33 @@
         copy.wait()
 
 
-def finish_kernel(*refs):
-    count = (len(refs) - 1) // 2
-    copies = [pltpu.make_async_copy(refs[i], refs[count + i], refs[-1].at[i]) for i in range(count)]
-    for copy in copies:
+def finish_kernel(hidden_in, grad_in, sums_in, hidden_out, grad_out, self_out, neigh_out,
+                  hidden_v, grad_v, sums_v, wide_v, sem):
+    arrive = [pltpu.make_async_copy(sums_in, sums_v, sem.at[0]),
+              pltpu.make_async_copy(hidden_in, hidden_v, sem.at[1]),
+              pltpu.make_async_copy(grad_in, grad_v, sem.at[2])]
+    leave = [pltpu.make_async_copy(wide_v.at[0], self_out, sem.at[3]),
+             pltpu.make_async_copy(wide_v.at[1], neigh_out, sem.at[4]),
+             pltpu.make_async_copy(hidden_v, hidden_out, sem.at[5]),
+             pltpu.make_async_copy(grad_v, grad_out, sem.at[6])]
+    for copy in arrive:
         copy.start()
-    for copy in copies:
+    arrive[0].wait()
+    wide_v[0] = sums_v[0].astype(F32)
+    leave[0].start()
+    wide_v[1] = sums_v[1].astype(F32)
+    leave[1].start()
+    arrive[1].wait()
+    leave[2].start()
+    arrive[2].wait()
+    leave[3].start()
+    for copy in leave:
         copy.wait()
-
-
-def live_keys(ids, counts):
-    live = jnp.arange(16, dtype=jnp.int32)[None, :] < counts[:, None]
-    return jnp.where(live, ids, BLOCKS).reshape(-1)
-
-
-def sort_slots(key):
-    slot = jnp.arange(128, dtype=jnp.int32)
-    full = key * 128 + slot
-    rank = jnp.sum((full[None, :] < full[:, None]).astype(jnp.int32), axis=1)
-    hit = rank[None, :] == slot[:, None]
-    order = jnp.sum(jnp.where(hit, slot[None, :], 0), axis=1)
-    before = rank[None, :] == slot[:, None] - 1
-    sorted_key = jnp.sum(jnp.where(hit, key[None, :], 0), axis=1)
-    prior_key = jnp.sum(jnp.where(before, key[None, :] + 1, 0), axis=1) - 1
-    same = (sorted_key == prior_key).astype(jnp.int32)
-    block = jnp.arange(256, dtype=jnp.int32)
-    upto = jnp.sum((key[None, :] <= block[:, None]).astype(jnp.int32), axis=1)
-    any_here = jnp.any(key[None, :] == block[:, None], axis=1)
-    last = jnp.where(any_here, upto - 1, 128)
-    return order, order // 16, same, last
 
 
 def shards(features, tile_ids, tile_count, tiles, self_weight, neigh_weight, bias, cotangent):
     feat_t = features[0].T
-    key = live_keys(tile_ids[0], tile_count[0])
     flat_tiles = tiles[0].reshape(128, EDGE, EDGE)
-    bias_here = lax.dynamic_slice_in_dim(bias, lax.axis_index("feat") * HID_ROWS, HID_ROWS)[None, :]
-
-    order, row, same, last = sort_slots(key)
     found = gather_messages(SPLIT_A)
     needs = [m.needs for m in found]
     steps = timed_order(found, needs, 1)
@@ -599,15 +630,15 @@
     results = (
         jax.ShapeDtypeStruct((SHARD_COLS, HID_ROWS), BF16),
         jax.ShapeDtypeStruct((FEAT_ROWS, SHARD_COLS), BF16),
-        jax.ShapeDtypeStruct((FEAT_ROWS, SHARD_COLS), F32),
-        jax.ShapeDtypeStruct((FEAT_ROWS, SHARD_COLS), F32),
+        jax.ShapeDtypeStruct((2, FEAT_ROWS, SHARD_COLS), BF16),
     )
+    wide = jax.ShapeDtypeStruct((FEAT_ROWS, SHARD_COLS), F32)
     held = pl.pallas_call(
         functools.partial(layer_kernel, found, steps, back_steps, offsets),
         name="layer",
         out_shape=results,
-        in_specs=[anywhere, smem, smem, smem, smem, smem, anywhere, anywhere, anywhere, vmem, anywhere],
-        out_specs=(anywhere,) * 4,
+        in_specs=[anywhere, smem, smem, anywhere, anywhere, anywhere, vmem, anywhere],
+        out_specs=(anywhere,) * 3,
         scratch_shapes=[
             pltpu.VMEM((BLOCKS + 1, FEAT_ROWS, EDGE), BF16),
             pltpu.VMEM((128, EDGE, EDGE), BF16),
@@ -631,11 +662,16 @@
             pltpu.VMEM((FEAT_ROWS, SHARD_COLS), F32),
             pltpu.VMEM((FEAT_ROWS, SHARD_COLS), F32),
             pltpu.VMEM((FEAT_ROWS, SHARD_COLS), BF16),
-            pltpu.VMEM((FEAT_ROWS, SHARD_COLS), F32),
-            pltpu.VMEM((3, 48, SHARD_COLS), F32),
-            pltpu.VMEM((7, 48, EDGE), F32),
+            pltpu.VMEM((2, FEAT_ROWS, SHARD_COLS), BF16),
+            pltpu.VMEM((FEAT_ROWS, SHARD_COLS), BF16),
+            pltpu.VMEM((FEAT_ROWS, SHARD_COLS), BF16),
+            pltpu.VMEM((3, 48, SHARD_COLS), BF16),
+            pltpu.VMEM((7, 48, EDGE), BF16),
             pltpu.VMEM((8, 48, EDGE), F32),
-            pltpu.VMEM((2, FEAT_ROWS, SHARD_COLS), F32),
+            pltpu.VMEM((8, 48, EDGE), BF16),
+            pltpu.VMEM((2, FEAT_ROWS, SHARD_COLS), BF16),
+            pltpu.VMEM((8, EDGE), jnp.int32),
+            pltpu.SMEM((8, EDGE), jnp.int32),
             dma((len(found),)), dma((len(found),)),
             dma((len(found),)), dma((len(found),)),
             dma((rings,)), dma((rings,)),
@@ -646,14 +682,20 @@
         compiler_params=pltpu.CompilerParams(
             collective_id=0, has_side_effects=True, vmem_limit_bytes=58 * 1024 * 1024),
         cost_estimate=pl.CostEstimate(flops=6 * 10**9, bytes_accessed=2 * 10**7, transcendentals=262144),
-    )(feat_t, key, order, row, same, last, flat_tiles, self_weight, neigh_weight, bias_here, cotangent[0])
+    )(feat_t, tile_ids[0], tile_count[0], flat_tiles, self_weight, neigh_weight, bias[None, :], cotangent[0])
     hidden, grad_t, self_grad, neigh_grad = pl.pallas_call(
         finish_kernel,
         name="finish",
-        out_shape=results,
-        in_specs=[anywhere] * 4,
+        out_shape=results[:2] + (wide, wide),
+        in_specs=[anywhere] * 3,
         out_specs=(anywhere,) * 4,
-        scratch_shapes=[dma((4,))],
+        scratch_shapes=[
+            pltpu.VMEM((SHARD_COLS, HID_ROWS), BF16),
+            pltpu.VMEM((FEAT_ROWS, SHARD_COLS), BF16),
+            pltpu.VMEM((2, FEAT_ROWS, SHARD_COLS), BF16),
+            pltpu.VMEM((2, FEAT_ROWS, SHARD_COLS), F32),
+            dma((7,)),
+        ],
     )(*held)
     return (hidden[None], grad_t.T[None], self_grad, neigh_grad)
 

time: 299 us -> 207 us (0.69)
  Pallas kernels: 293 us -> 206 us
  other arithmetic: 3.1 us -> 0 us
    pallas_call x1, Pallas kernels: 76.6 us -> 2.68 us  [shards(): pl.pallas_call(finish_kernel, name='finish', out_shape=results[:2] + (wid...]
    pallas_call x1, Pallas kernels: 216 us -> 204 us  [shards(): pl.pallas_call(functools.partial(layer_kernel, found, steps, back_steps,...]
where the time goes in v3:
time: 207 us
  Pallas kernels  206 us (100%)
    pallas_call x1, Pallas kernels, shards(): pl.pallas_call(functools.partial(layer_kernel, found, steps, back_steps,...  204 us

profile of v3, /device:TPU:8, one launch (start us, length us, event | category | flops | bytes accessed | tf_op | source)
XLA Modules:
  0.0 206.9 jit_solution(2248167667613922219)
XLA Ops:
  0.6 203.6 %layer.1 = (bf16[1024,256]{1,0:T(8,128)(2,1)}, bf16[192,1024]{1,0:T(8,128)(2,1)}, bf16[2,192,1024]{2,1,0:T(8,128)(2,1)}) custom-call(bf16[192,1024]{1,0:T(8,128)(2,1)} %bitcast.15, s32[8,16]{1,0:T(8,128)} %bitcast.17, s32[8]{0:T(128)} %bitcast.19, bf16[128,128,128]{2,1,0:T(8,128)(2,1)} %bitcast.12, bf16[192,1024]{1,0:T(8,128)(2,1)} %ws_hbm.1, ...), custom_call_target="tpu_custom_call" | custom-call | flops 6000000000 | bytes 20000000 | tf_op jit(solution)/shard_map/layer/pallas_call | solution.py:636
  204.2 2.7 %finish.1 = (bf16[1024,256]{1,0:T(8,128)(2,1)}, bf16[192,1024]{1,0:T(8,128)(2,1)}, f32[192,1024]{1,0:T(8,128)}, f32[192,1024]{1,0:T(8,128)}) custom-call(bf16[1024,256]{1,0:T(8,128)(2,1)} %get-tuple-element.11.hidden_in, bf16[192,1024]{1,0:T(8,128)(2,1)} %get-tuple-element.12.grad_in, bf16[2,192,1024]{2,1,0:T(8,128)(2,1)} %get-tuple-element.13.sums_in), custom_call_target="tpu_custom_call" | custom-call | tf_op jit(solution)/shard_map/finish/pallas_call | solution.py:686

commit v4 on v3

--- a/solution.py
+++ b/solution.py
@@ -22,6 +22,8 @@
 CHUNKS = 4
 CHUNK_COLS = SHARD_COLS // CHUNKS
 SPLIT_A = 80
+LIMIT = 3
+DELAY = 30.0
 
 
 class Message:
@@ -81,13 +83,12 @@
 
     def longest(i):
         if not depth[i]:
-            depth[i] = found[i].size + max([longest(j) for j in followers[i]], default=0)
+            depth[i] = found[i].size + DELAY + max([longest(j) for j in followers[i]], default=0)
         return depth[i]
 
     for i in range(count):
         longest(i)
-    waiting = {}
-    busy = {}
+    queue, flying, free = {}, {}, {}
     events = []
     steps = []
     tick = [0]
@@ -96,25 +97,39 @@
         tick[0] += 1
         heapq.heappush(events, (when, tick[0], kind, what))
 
-    def offer(i, when):
-        steps.append(("send", i))
-        link = (found[i].axis, found[i].way * towards)
-        start = max(when, busy.get(link, 0.0))
-        busy[link] = start + found[i].size
-        push(busy[link] + 30.0, "recv", i)
-
-    for i in sorted((i for i in range(count) if missing[i] == 0), key=lambda i: -depth[i]):
-        offer(i, 0.0)
+    def link_of(i):
+        return (found[i].axis, found[i].way * towards)
+
+    def feed(link, when):
+        while queue.get(link) and flying.get(link, 0) < LIMIT:
+            i = min(queue[link], key=lambda k: (-depth[k], k))
+            queue[link].remove(i)
+            flying[link] = flying.get(link, 0) + 1
+            steps.append(("send", i))
+            free[link] = max(when, free.get(link, 0.0)) + found[i].size
+            push(free[link], "sent", i)
+            push(free[link] + DELAY, "recv", i)
+
+    for i in range(count):
+        if missing[i] == 0:
+            queue.setdefault(link_of(i), []).append(i)
+    for link in list(queue):
+        feed(link, 0.0)
     while events:
         when, _, kind, what = heapq.heappop(events)
-        steps.append(("recv", what))
-        ready = []
-        for j in followers[what]:
-            missing[j] -= 1
-            if missing[j] == 0:
-                ready.append(j)
-        for j in sorted(ready, key=lambda j: -depth[j]):
-            offer(j, when)
+        steps.append((kind, what))
+        touched = []
+        if kind == "sent":
+            flying[link_of(what)] -= 1
+            touched.append(link_of(what))
+        else:
+            for j in followers[what]:
+                missing[j] -= 1
+                if missing[j] == 0:
+                    queue.setdefault(link_of(j), []).append(j)
+                    touched.append(link_of(j))
+        for link in touched:
+            feed(link, when)
     return steps
 
 
@@ -181,8 +196,8 @@
 def layer_kernel(found, steps, back_steps, offsets, feat_hbm, ids_ref, count_ref,
                  tiles_hbm, ws_hbm, wn_hbm, bias_ref, cot_hbm,
                  hidden_hbm, grad_hbm, sums_hbm,
-                 table, tiles_v, ws_v, wn_v, cot_v, hidden_v, feat_all, ws_all, wn_all, ws_t, wn_t,
-                 neigh_all, slope_all, self_pre, cot_t,
+                 table, tiles_v, feat_own, feat_q, ws_full, wn_full, cot_v, cot_q, hidden_v, hidden_q,
+                 neigh_own, neigh_q, slope_all, self_pre, back_out,
                  back_v, seg, landed, grad_v, sums, total_v, grad_v16,
                  half_v, half_sums, first_in, second_in, third_in, third_v, third_half, final_v, plan_v, plan,
                  ag_send, ag_recv, rs_send, rs_recv, y_send, y_recv, w_send, w_recv, ar_send, ar_recv, local_sem):
@@ -200,15 +215,21 @@
     for step in range(1, RING_Y):
         pl.semaphore_signal(barrier, inc=1, device_id={"feat": lax.rem(me_y + step, RING_Y)}, device_id_type=MESH)
 
-    mine_h = pl.ds(pl.multiple_of(me_y * HID_ROWS, HID_ROWS), HID_ROWS)
+    def feature_rows(owner, low, size):
+        return pl.ds(pl.multiple_of(owner * FEAT_ROWS + low, 16), size)
+
+    def quarter(owner):
+        return pl.ds(pl.multiple_of(owner * CHUNK_COLS, CHUNK_COLS), CHUNK_COLS)
+
     own = [pltpu.make_async_copy(feat_hbm.at[:, pl.ds(part * EDGE, EDGE)], table.at[vert * 8 + part],
                                  local_sem.at[part]) for part in range(8)]
     inputs = [
-        pltpu.make_async_copy(feat_hbm, feat_all.at[me_y], local_sem.at[8]),
-        pltpu.make_async_copy(ws_hbm, ws_v, local_sem.at[9]),
-        pltpu.make_async_copy(wn_hbm, wn_v, local_sem.at[10]),
-        pltpu.make_async_copy(ws_hbm.at[:, mine_h], ws_all.at[me_y], local_sem.at[11]),
-        pltpu.make_async_copy(wn_hbm.at[:, mine_h], wn_all.at[me_y], local_sem.at[12]),
+        pltpu.make_async_copy(feat_hbm, feat_own, local_sem.at[8]),
+        pltpu.make_async_copy(ws_hbm, ws_full.at[feature_rows(me_y, 0, FEAT_ROWS), :], local_sem.at[9]),
+        pltpu.make_async_copy(wn_hbm, wn_full.at[feature_rows(me_y, 0, FEAT_ROWS), :], local_sem.at[10]),
+        pltpu.make_async_copy(feat_hbm.at[:, quarter(me_y)], feat_q.at[feature_rows(me_y, 0, FEAT_ROWS), :],
+                              local_sem.at[11]),
+        pltpu.make_async_copy(cot_hbm.at[quarter(me_y), :], cot_q.at[me_y], local_sem.at[12]),
         pltpu.make_async_copy(cot_hbm, cot_v, local_sem.at[13]),
         pltpu.make_async_copy(tiles_hbm, tiles_v, local_sem.at[14]),
     ]
@@ -229,39 +250,49 @@
             src_ref=part, dst_ref=part, send_sem=ag_send.at[i], recv_sem=ag_recv.at[i],
             device_id={"vert": to}, device_id_type=MESH)
 
-    feat_ring = YRing(y_send, y_recv, 0, lambda o, low, size: feat_all.at[o, pl.ds(low, size), :],
-                      FEAT_ROWS, me_y)
-
-    def weight_copy(which, step):
-        source, target = ((ws_v, ws_all), (wn_v, wn_all))[which]
+    ws_ring = YRing(y_send, y_recv, 0, lambda o, low, size: ws_full.at[feature_rows(o, low, size), :],
+                    FEAT_ROWS, me_y)
+    wn_ring = YRing(y_send, y_recv, 4, lambda o, low, size: wn_full.at[feature_rows(o, low, size), :],
+                    FEAT_ROWS, me_y)
+    slope_ring = YRing(y_send, y_recv, 8, lambda o, low, size: slope_all.at[o, pl.ds(low, size), :],
+                       CHUNK_COLS, me_y)
+
+    exchanges = (
+        (lambda p: feat_own.at[:, quarter(p)], lambda o: feat_q.at[feature_rows(o, 0, FEAT_ROWS), :]),
+        (lambda p: cot_v.at[quarter(p), :], lambda o: cot_q.at[o]),
+        (lambda p: neigh_own.at[p], lambda o: neigh_q.at[feature_rows(o, 0, FEAT_ROWS), :]),
+        (lambda p: back_out.at[p], lambda o: back_v.at[pl.ds(o * 2, 2)]),
+        (lambda p: hidden_q.at[:, quarter(p)], lambda o: hidden_v.at[quarter(o), :]),
+    )
+    FEATS, COTS, NEIGHS, BACKS, HIDDENS = range(5)
+
+    def hand_over(which, step):
+        piece, place = exchanges[which]
         to = lax.rem(me_y + step, RING_Y)
-        place = which * 3 + step - 1
+        number = which * 3 + step - 1
         return pltpu.make_async_remote_copy(
-            src_ref=source.at[:, pl.ds(pl.multiple_of(to * HID_ROWS, HID_ROWS), HID_ROWS)],
-            dst_ref=target.at[me_y],
-            send_sem=w_send.at[place], recv_sem=w_recv.at[place],
+            src_ref=piece(to), dst_ref=place(me_y), send_sem=w_send.at[number], recv_sem=w_recv.at[number],
             device_id={"feat": to}, device_id_type=MESH)
 
-    def weight_arrival(which, step):
-        source, target = ((ws_v, ws_all), (wn_v, wn_all))[which]
-        place = which * 3 + step - 1
-        return pltpu.make_async_remote_copy(
-            src_ref=source.at[:, pl.ds(0, HID_ROWS)],
-            dst_ref=target.at[lax.rem(me_y - step + RING_Y, RING_Y)],
-            send_sem=w_send.at[place], recv_sem=w_recv.at[place],
-            device_id={"feat": lax.rem(me_y + step, RING_Y)}, device_id_type=MESH)
+    def take_over(which):
+        place = exchanges[which][1]
+        for step in range(1, RING_Y):
+            number = which * 3 + step - 1
+            here = place(lax.rem(me_y - step + RING_Y, RING_Y))
+            pltpu.make_async_remote_copy(
+                src_ref=here, dst_ref=here, send_sem=w_send.at[number], recv_sem=w_recv.at[number],
+                device_id={"feat": lax.rem(me_y + step, RING_Y)}, device_id_type=MESH).wait_recv()
 
     def prepare_start():
         for copy in inputs:
             copy.wait()
-        feat_ring.start()
-        for which in (0, 1):
-            for step in range(1, RING_Y):
-                weight_copy(which, step).start()
+        for step in (2, 1, 3):
+            hand_over(FEATS, step).start()
+        ws_ring.start()
+        wn_ring.start()
+        for step in (2, 1, 3):
+            hand_over(COTS, step).start()
         table[BLOCKS] = jnp.zeros((FEAT_ROWS, EDGE), BF16)
-        for c in range(CHUNKS):
-            span = pl.ds(c * CHUNK_COLS, CHUNK_COLS)
-            cot_t[:, span] = dot_rows(unit(HID_ROWS), cot_v[span, :]).astype(BF16)
 
     plan_copy = pltpu.make_async_copy(plan_v, plan, local_sem.at[17])
 
@@ -300,43 +331,36 @@
         plan_v[6:8, :] = jnp.zeros((2, EDGE), jnp.int32)
         plan_copy.start()
 
-    def prepare_weights():
-        for which in (0, 1):
-            for step in range(1, RING_Y):
-                weight_arrival(which, step).wait_recv()
-        for y in range(RING_Y):
-            ws_t[y] = dot_rows(unit(HID_ROWS), ws_all[y]).astype(BF16)
-            wn_t[y] = dot_rows(unit(HID_ROWS), wn_all[y]).astype(BF16)
-
-    def prepare_self(c):
-        span = pl.ds(c * CHUNK_COLS, CHUNK_COLS)
-        total = jnp.concatenate([jnp.broadcast_to(bias_ref[:, mine_h], (EDGE, HID_ROWS)).T] * (CHUNK_COLS // EDGE), axis=1)
-        for y in range(RING_Y):
-            total = total + dot_plain(ws_t[y], feat_all[y, :, span])
-        self_pre[:, span] = total
-
-    side = {4: prepare_plan, 8: prepare_start, 12: plan_copy.wait, 16: feat_ring.hand_on, 20: prepare_weights, 24: feat_ring.finish}
-    for c in range(CHUNKS):
-        side[30 + 6 * c] = functools.partial(prepare_self, c)
+    def hand_on_weights():
+        ws_ring.hand_on()
+        wn_ring.hand_on()
+
+    def finish_weights():
+        ws_ring.finish()
+        wn_ring.finish()
+        take_over(FEATS)
+
+    def prepare_self(part):
+        span = slice(part * HID_ROWS, (part + 1) * HID_ROWS)
+        turned = dot_rows(unit(CHUNK_COLS), feat_q[...]).astype(BF16)
+        self_pre[:, span] = dot_plain(turned, ws_full[:, span]) + bias_ref[:, span]
+
+    side = {4: prepare_plan, 8: prepare_start, 12: plan_copy.wait, 34: hand_on_weights, 48: finish_weights,
+            68: lambda: take_over(COTS)}
+    for part in range(RING_Y):
+        side[52 + 4 * part] = functools.partial(prepare_self, part)
 
     arrived = 0
     for kind, i in steps:
         if kind == "send":
             forward_message(i, True).start()
+        elif kind == "sent":
+            forward_message(i, True).wait_send()
         else:
             forward_message(i, False).wait_recv()
             arrived += 1
             if arrived in side:
                 side[arrived]()
-
-    neigh_rings = [
-        YRing(y_send, y_recv, 4 + 4 * c,
-              lambda o, low, size, c=c: neigh_all.at[o, c, pl.ds(low, size), :], FEAT_ROWS, me_y)
-        for c in range(CHUNKS)]
-    slope_rings = [
-        YRing(y_send, y_recv, 4 + 4 * CHUNKS + 4 * c,
-              lambda o, low, size, c=c: slope_all.at[o, c, pl.ds(low, size), :], HID_ROWS, me_y)
-        for c in range(CHUNKS)]
 
     def aggregate(b):
         total = jnp.zeros((FEAT_ROWS, EDGE), F32)
@@ -348,44 +372,40 @@
             total = total + dot_rows(jnp.concatenate(left, axis=1), jnp.concatenate(right, axis=1))
         return total.astype(BF16)
 
-    per_chunk = CHUNK_COLS // EDGE
-    for c in range(CHUNKS):
-        for part in range(per_chunk):
-            neigh_all[me_y, c, :, part * EDGE:(part + 1) * EDGE] = aggregate(c * per_chunk + part)
-        neigh_rings[c].start()
-        if c:
-            neigh_rings[c - 1].hand_on()
-    neigh_rings[CHUNKS - 1].hand_on()
-
-    for c in range(CHUNKS):
-        span = pl.ds(c * CHUNK_COLS, CHUNK_COLS)
-        neigh_rings[c].finish()
-        value = self_pre[:, span]
-        for y in range(RING_Y):
-            value = value + dot_plain(wn_t[y], neigh_all[y, c])
+    for step in (2, 1, 3, 0):
+        owner = lax.rem(me_y + step, RING_Y)
+        for part in range(2):
+            neigh_own[owner, :, part * EDGE:(part + 1) * EDGE] = aggregate(owner * 2 + part)
+        if step:
+            hand_over(NEIGHS, step).start()
+        else:
+            neigh_q[feature_rows(me_y, 0, FEAT_ROWS), :] = neigh_own[me_y]
+    take_over(NEIGHS)
+
+    turned = dot_rows(unit(CHUNK_COLS), neigh_q[...]).astype(BF16)
+    for part in range(RING_Y):
+        span = slice(part * HID_ROWS, (part + 1) * HID_ROWS)
+        value = self_pre[:, span] + dot_plain(turned, wn_full[:, span])
         sigmoid = jax.nn.sigmoid(value)
-        slope = cot_t[:, span].astype(F32) * (sigmoid * (1.0 + value * (1.0 - sigmoid)))
-        slope_all[me_y, c] = slope.astype(BF16)
-        slope_rings[c].start()
-        if c:
-            slope_rings[c - 1].hand_on()
-        hidden_t = (value * sigmoid).astype(BF16)
-        for part in range(per_chunk):
-            hidden_v[pl.ds(c * CHUNK_COLS + part * EDGE, EDGE), :] = dot_rows(
-                unit(EDGE), hidden_t[:, part * EDGE:(part + 1) * EDGE]).astype(BF16)
-    slope_rings[CHUNKS - 1].hand_on()
-    hidden_out = pltpu.make_async_copy(hidden_v, hidden_hbm, local_sem.at[15])
-    hidden_out.start()
-    for c in range(CHUNKS):
-        slope_rings[c].finish()
-        value = jnp.zeros((FEAT_ROWS, CHUNK_COLS), F32)
-        for y in range(RING_Y):
-            value = value + dot_plain(wn_v[:, y * HID_ROWS:(y + 1) * HID_ROWS], slope_all[y, c])
-        value = value.astype(BF16)
-        for part in range(per_chunk):
-            back_v[c * per_chunk + part] = value[:, part * EDGE:(part + 1) * EDGE]
-    for i in range(len(found)):
-        forward_message(i, True).wait_send()
+        slope = cot_q[part].astype(F32) * (sigmoid * (1.0 + value * (1.0 - sigmoid)))
+        slope_all[me_y, :, span] = slope.astype(BF16)
+        hidden_q[:, span] = (value * sigmoid).astype(BF16)
+    for step in (2, 1, 3, 0):
+        owner = lax.rem(me_y + step, RING_Y)
+        back = dot_rows(wn_full[feature_rows(owner, 0, FEAT_ROWS), :], slope_all[me_y]).astype(BF16)
+        for part in range(2):
+            piece = back[:, part * EDGE:(part + 1) * EDGE]
+            if step:
+                back_out[owner, part] = piece
+            else:
+                back_v[me_y * 2 + part] = piece
+        if step:
+            hand_over(BACKS, step).start()
+    slope_ring.start()
+    for step in (2, 1, 3):
+        hand_over(HIDDENS, step).start()
+    hidden_v[quarter(me_y), :] = hidden_q[:, quarter(me_y)]
+    take_over(BACKS)
 
     seg[128] = jnp.zeros((FEAT_ROWS, EDGE), BF16)
 
@@ -409,6 +429,9 @@
         return carry
 
     lax.fori_loop(0, RING_X * RING_Z, fill, 0)
+    for part in range(8):
+        total_v[:, part * EDGE:(part + 1) * EDGE] = table[vert * 8 + part].astype(F32)
+    hidden_out = pltpu.make_async_copy(hidden_v, hidden_hbm, local_sem.at[15])
 
     def message(i):
         m = found[i]
@@ -482,14 +505,15 @@
         return copy_to(target, target, number, axis, 1)
 
     def weight_sums():
-        for y in range(RING_Y):
-            span = slice(y * HID_ROWS, (y + 1) * HID_ROWS)
+        slope_ring.finish()
+        for part in range(RING_Y):
+            span = slice(part * HID_ROWS, (part + 1) * HID_ROWS)
             one = jnp.zeros((FEAT_ROWS, HID_ROWS), F32)
             two = jnp.zeros((FEAT_ROWS, HID_ROWS), F32)
-            for c in range(CHUNKS):
-                piece = slope_all[y, c]
-                one = one + dot_rows(feat_all[me_y, :, c * CHUNK_COLS:(c + 1) * CHUNK_COLS], piece)
-                two = two + dot_rows(neigh_all[me_y, c], piece)
+            for q in range(RING_Y):
+                piece = slope_all[q, :, span]
+                one = one + dot_plain(feat_own[:, q * CHUNK_COLS:(q + 1) * CHUNK_COLS], piece)
+                two = two + dot_plain(neigh_own[q], piece)
             grad_v[0, :, span] = one
             grad_v[1, :, span] = two
             half_v[0, :, span] = one.astype(BF16)
@@ -497,13 +521,14 @@
         swap_rep().start()
 
     def own_total():
-        for c in range(CHUNKS):
-            span = slice(c * CHUNK_COLS, (c + 1) * CHUNK_COLS)
-            value = jnp.concatenate(
-                [table[vert * 8 + c * per_chunk + part] for part in range(per_chunk)], axis=1).astype(F32)
-            for y in range(RING_Y):
-                value = value + dot_plain(ws_v[:, y * HID_ROWS:(y + 1) * HID_ROWS], slope_all[y, c])
-            total_v[:, span] = value
+        weight = ws_full[feature_rows(me_y, 0, FEAT_ROWS), :]
+        for q in range(RING_Y):
+            span = slice(q * CHUNK_COLS, (q + 1) * CHUNK_COLS)
+            total_v[:, span] = total_v[:, span] + dot_rows(weight, slope_all[q])
+
+    def hidden_leave():
+        take_over(HIDDENS)
+        hidden_out.start()
 
     def after_rep():
         landing(first_in, 0, "rep").wait_recv()
@@ -545,8 +570,8 @@
             landing(final_v.at[rep, final_rows(lax.rem(x - step + RING_X, RING_X)), :], 17 + step, "x").wait_recv()
         share_rep().start()
 
-    side = {0: lambda: (weight_sums(), own_total()), 4: after_rep, 18: after_x, 32: after_z,
-            46: gathered_z, 60: gathered_x}
+    side = {6: slope_ring.hand_on, 14: weight_sums, 16: own_total, 20: after_rep, 30: hidden_leave, 34: after_x,
+            48: after_z, 61: gathered_z, 73: gathered_x}
     arrived = 0
     for kind, i in back_steps:
         if kind == "recv":
@@ -555,6 +580,8 @@
             message(i).wait_recv()
             absorb(i)
             arrived += 1
+        elif kind == "sent":
+            message(i).wait_send()
         else:
             message(i).start()
 
@@ -565,8 +592,6 @@
     grad_v16[...] = total_v[...].astype(BF16)
     outputs.append(pltpu.make_async_copy(grad_v16, grad_hbm, local_sem.at[16]))
     outputs[-1].start()
-    for i in range(len(found)):
-        message(i).wait_send()
     swap_rep().wait_send()
     for step in range(1, RING_X):
         scatter_x(step).wait_send()
@@ -575,12 +600,11 @@
         scatter_z(step).wait_send()
         gather_z(step).wait_send()
     share_rep().wait_send()
-    feat_ring.drain()
-    for which in (0, 1):
+    for ring in (ws_ring, wn_ring, slope_ring):
+        ring.drain()
+    for which in range(5):
         for step in range(1, RING_Y):
-            weight_copy(which, step).wait_send()
-    for ring in neigh_rings + slope_rings:
-        ring.drain()
+            hand_over(which, step).wait_send()
     hidden_out.wait()
     for copy in outputs:
         copy.wait()
@@ -626,7 +650,6 @@
     smem = pl.BlockSpec(memory_space=pltpu.SMEM)
     anywhere = pl.BlockSpec(memory_space=pl.ANY)
     dma = pltpu.SemaphoreType.DMA
-    rings = 4 + 8 * CHUNKS
     results = (
         jax.ShapeDtypeStruct((SHARD_COLS, HID_ROWS), BF16),
         jax.ShapeDtypeStruct((FEAT_ROWS, SHARD_COLS), BF16),
@@ -643,18 +666,18 @@
             pltpu.VMEM((BLOCKS + 1, FEAT_ROWS, EDGE), BF16),
             pltpu.VMEM((128, EDGE, EDGE), BF16),
             pltpu.VMEM((FEAT_ROWS, SHARD_COLS), BF16),
-            pltpu.VMEM((FEAT_ROWS, SHARD_COLS), BF16),
+            pltpu.VMEM((RING_Y * FEAT_ROWS, CHUNK_COLS), BF16),
+            pltpu.VMEM((RING_Y * FEAT_ROWS, SHARD_COLS), BF16),
+            pltpu.VMEM((RING_Y * FEAT_ROWS, SHARD_COLS), BF16),
             pltpu.VMEM((SHARD_COLS, HID_ROWS), BF16),
+            pltpu.VMEM((RING_Y, CHUNK_COLS, HID_ROWS), BF16),
             pltpu.VMEM((SHARD_COLS, HID_ROWS), BF16),
-            pltpu.VMEM((RING_Y, FEAT_ROWS, SHARD_COLS), BF16),
-            pltpu.VMEM((RING_Y, FEAT_ROWS, HID_ROWS), BF16),
-            pltpu.VMEM((RING_Y, FEAT_ROWS, HID_ROWS), BF16),
-            pltpu.VMEM((RING_Y, HID_ROWS, FEAT_ROWS), BF16),
-            pltpu.VMEM((RING_Y, HID_ROWS, FEAT_ROWS), BF16),
-            pltpu.VMEM((RING_Y, CHUNKS, FEAT_ROWS, CHUNK_COLS), BF16),
-            pltpu.VMEM((RING_Y, CHUNKS, HID_ROWS, CHUNK_COLS), BF16),
-            pltpu.VMEM((HID_ROWS, SHARD_COLS), F32),
-            pltpu.VMEM((HID_ROWS, SHARD_COLS), BF16),
+            pltpu.VMEM((CHUNK_COLS, SHARD_COLS), BF16),
+            pltpu.VMEM((RING_Y, FEAT_ROWS, CHUNK_COLS), BF16),
+            pltpu.VMEM((RING_Y * FEAT_ROWS, CHUNK_COLS), BF16),
+            pltpu.VMEM((RING_Y, CHUNK_COLS, SHARD_COLS), BF16),
+            pltpu.VMEM((CHUNK_COLS, SHARD_COLS), F32),
+            pltpu.VMEM((RING_Y, 2, FEAT_ROWS, EDGE), BF16),
             pltpu.VMEM((8, FEAT_ROWS, EDGE), BF16),
             pltpu.VMEM((129, FEAT_ROWS, EDGE), BF16),
             pltpu.VMEM((8, at, EDGE), BF16),
@@ -674,8 +697,8 @@
             pltpu.SMEM((8, EDGE), jnp.int32),
             dma((len(found),)), dma((len(found),)),
             dma((len(found),)), dma((len(found),)),
-            dma((rings,)), dma((rings,)),
-            dma((6,)), dma((6,)),
+            dma((12,)), dma((12,)),
+            dma((15,)), dma((15,)),
             dma((22,)), dma((22,)),
             dma((19,)),
         ],

time: 207 us -> 181 us (0.87)
  Pallas kernels: 206 us -> 179 us
    pallas_call x1, Pallas kernels: 204 us -> 176 us  [shards(): pl.pallas_call(functools.partial(layer_kernel, found, steps, back_steps,...]
where the time goes in v4:
time: 181 us; the launch traced here: 179 us
  Pallas kernels  179 us (99%)
    pallas_call x1, Pallas kernels, shards(): pl.pallas_call(functools.partial(layer_kernel, found, steps, back_steps,...  176 us

profile of v4, /device:TPU:8, one launch (start us, length us, event | category | flops | bytes accessed | tf_op | source)
XLA Modules:
  0.0 179.3 jit_solution(9522099062176833412)
XLA Ops:
  0.6 176.0 %layer.1 = (bf16[1024,256]{1,0:T(8,128)(2,1)}, bf16[192,1024]{1,0:T(8,128)(2,1)}, bf16[2,192,1024]{2,1,0:T(8,128)(2,1)}) custom-call(bf16[192,1024]{1,0:T(8,128)(2,1)} %bitcast.15, s32[8,16]{1,0:T(8,128)} %bitcast.17, s32[8]{0:T(128)} %bitcast.19, bf16[128,128,128]{2,1,0:T(8,128)(2,1)} %bitcast.12, bf16[192,1024]{1,0:T(8,128)(2,1)} %ws_hbm.1, ...), custom_call_target="tpu_custom_call" | custom-call | flops 6000000000 | bytes 20000000 | tf_op jit(solution)/shard_map/layer/pallas_call | solution.py:659
  176.7 2.7 %finish.1 = (bf16[1024,256]{1,0:T(8,128)(2,1)}, bf16[192,1024]{1,0:T(8,128)(2,1)}, f32[192,1024]{1,0:T(8,128)}, f32[192,1024]{1,0:T(8,128)}) custom-call(bf16[1024,256]{1,0:T(8,128)(2,1)} %get-tuple-element.11.hidden_in, bf16[192,1024]{1,0:T(8,128)(2,1)} %get-tuple-element.12.grad_in, bf16[2,192,1024]{2,1,0:T(8,128)(2,1)} %get-tuple-element.13.sums_in), custom_call_target="tpu_custom_call" | custom-call | tf_op jit(solution)/shard_map/finish/pallas_call | solution.py:709

commit v5 on v4

--- a/solution.py
+++ b/solution.py
@@ -199,7 +199,7 @@
                  table, tiles_v, feat_own, feat_q, ws_full, wn_full, cot_v, cot_q, hidden_v, hidden_q,
                  neigh_own, neigh_q, slope_all, self_pre, back_out,
                  back_v, seg, landed, grad_v, sums, total_v, grad_v16,
-                 half_v, half_sums, first_in, second_in, third_in, third_v, third_half, final_v, plan_v, plan,
+                 half_v, half_sums, first_in, relay_in, second_in, third_in, third_v, third_half, final_v, plan_v, plan,
                  ag_send, ag_recv, rs_send, rs_recv, y_send, y_recv, w_send, w_recv, ar_send, ar_recv, local_sem):
     vert = lax.axis_index("vert")
     rep = lax.axis_index("rep")
@@ -260,11 +260,13 @@
     exchanges = (
         (lambda p: feat_own.at[:, quarter(p)], lambda o: feat_q.at[feature_rows(o, 0, FEAT_ROWS), :]),
         (lambda p: cot_v.at[quarter(p), :], lambda o: cot_q.at[o]),
-        (lambda p: neigh_own.at[p], lambda o: neigh_q.at[feature_rows(o, 0, FEAT_ROWS), :]),
-        (lambda p: back_out.at[p], lambda o: back_v.at[pl.ds(o * 2, 2)]),
+        (lambda p: neigh_own.at[p, 0], lambda o: neigh_q.at[0, feature_rows(o, 0, FEAT_ROWS), :]),
+        (lambda p: neigh_own.at[p, 1], lambda o: neigh_q.at[1, feature_rows(o, 0, FEAT_ROWS), :]),
+        (lambda p: back_out.at[p, 0], lambda o: back_v.at[o * 2]),
+        (lambda p: back_out.at[p, 1], lambda o: back_v.at[o * 2 + 1]),
         (lambda p: hidden_q.at[:, quarter(p)], lambda o: hidden_v.at[quarter(o), :]),
     )
-    FEATS, COTS, NEIGHS, BACKS, HIDDENS = range(5)
+    FEATS, COTS, NEIGHS, BACKS, HIDDENS = 0, 1, 2, 4, 6
 
     def hand_over(which, step):
         piece, place = exchanges[which]
@@ -372,40 +374,40 @@
             total = total + dot_rows(jnp.concatenate(left, axis=1), jnp.concatenate(right, axis=1))
         return total.astype(BF16)
 
-    for step in (2, 1, 3, 0):
-        owner = lax.rem(me_y + step, RING_Y)
-        for part in range(2):
-            neigh_own[owner, :, part * EDGE:(part + 1) * EDGE] = aggregate(owner * 2 + part)
-        if step:
-            hand_over(NEIGHS, step).start()
-        else:
-            neigh_q[feature_rows(me_y, 0, FEAT_ROWS), :] = neigh_own[me_y]
-    take_over(NEIGHS)
-
-    turned = dot_rows(unit(CHUNK_COLS), neigh_q[...]).astype(BF16)
-    for part in range(RING_Y):
-        span = slice(part * HID_ROWS, (part + 1) * HID_ROWS)
-        value = self_pre[:, span] + dot_plain(turned, wn_full[:, span])
-        sigmoid = jax.nn.sigmoid(value)
-        slope = cot_q[part].astype(F32) * (sigmoid * (1.0 + value * (1.0 - sigmoid)))
-        slope_all[me_y, :, span] = slope.astype(BF16)
-        hidden_q[:, span] = (value * sigmoid).astype(BF16)
-    for step in (2, 1, 3, 0):
-        owner = lax.rem(me_y + step, RING_Y)
-        back = dot_rows(wn_full[feature_rows(owner, 0, FEAT_ROWS), :], slope_all[me_y]).astype(BF16)
-        for part in range(2):
-            piece = back[:, part * EDGE:(part + 1) * EDGE]
+    for part in range(2):
+        for step in (2, 1, 3, 0):
+            owner = lax.rem(me_y + step, RING_Y)
+            neigh_own[owner, part] = aggregate(owner * 2 + part)
             if step:
-                back_out[owner, part] = piece
+                hand_over(NEIGHS + part, step).start()
             else:
-                back_v[me_y * 2 + part] = piece
-        if step:
-            hand_over(BACKS, step).start()
+                neigh_q[part, feature_rows(me_y, 0, FEAT_ROWS), :] = neigh_own[me_y, part]
+
+    for part in range(2):
+        take_over(NEIGHS + part)
+        rows_here = slice(part * EDGE, (part + 1) * EDGE)
+        turned = dot_rows(unit(EDGE), neigh_q[part]).astype(BF16)
+        for hid in range(RING_Y):
+            span = slice(hid * HID_ROWS, (hid + 1) * HID_ROWS)
+            value = self_pre[rows_here, span] + dot_plain(turned, wn_full[:, span])
+            sigmoid = jax.nn.sigmoid(value)
+            slope = cot_q[hid, rows_here, :].astype(F32) * (sigmoid * (1.0 + value * (1.0 - sigmoid)))
+            slope_all[me_y, rows_here, span] = slope.astype(BF16)
+            hidden_q[rows_here, span] = (value * sigmoid).astype(BF16)
+        for step in (2, 1, 3, 0):
+            owner = lax.rem(me_y + step, RING_Y)
+            back = dot_rows(wn_full[feature_rows(owner, 0, FEAT_ROWS), :], slope_all[me_y, rows_here, :]).astype(BF16)
+            if step:
+                back_out[owner, part] = back
+                hand_over(BACKS + part, step).start()
+            else:
+                back_v[me_y * 2 + part] = back
     slope_ring.start()
     for step in (2, 1, 3):
         hand_over(HIDDENS, step).start()
     hidden_v[quarter(me_y), :] = hidden_q[:, quarter(me_y)]
     take_over(BACKS)
+    take_over(BACKS + 1)
 
     seg[128] = jnp.zeros((FEAT_ROWS, EDGE), BF16)
 
@@ -482,49 +484,63 @@
     def swap_rep():
         return copy_to(half_v.at[1 - rep], first_in, 0, "rep", 0)
 
-    def scatter_x(step):
-        to = lax.rem(x + step, RING_X)
-        return copy_to(half_sums.at[pl.ds(pl.multiple_of(to * 48, 48), 48), :], second_in.at[step - 1], step, "x", step)
+    HALF = SHARD_COLS // 2
+
+    def half_lanes(way):
+        return pl.ds(0 if way == 1 else HALF, HALF)
+
+    def relay_x(way):
+        to = lax.rem(x + 2, RING_X)
+        number = 1 if way == 1 else 2
+        return copy_to(half_sums.at[final_rows(to), half_lanes(way)], relay_in.at[number - 1], number, "x", way)
+
+    def scatter_x(way):
+        to = lax.rem(x + way + RING_X, RING_X)
+        number = 3 if way == 1 else 4
+        return copy_to(half_sums.at[final_rows(to), :], second_in.at[number - 3], number, "x", way)
 
     def scatter_z(step):
         to = lax.rem(z + step, RING_Z)
-        return copy_to(third_half.at[to], third_in.at[step - 1], 3 + step, "z", step)
+        return copy_to(third_half.at[to], third_in.at[step - 1], 4 + step, "z", step)
 
     def gather_z(step):
         mine = final_v.at[rep, final_rows(x), final_lanes(z)]
-        return copy_to(mine, mine, 10 + step, "z", step)
-
-    def gather_x(step):
+        return copy_to(mine, mine, 11 + step, "z", step)
+
+    def gather_x(way):
         mine = final_v.at[rep, final_rows(x), :]
-        return copy_to(mine, mine, 17 + step, "x", step)
+        return copy_to(mine, mine, 19 if way == 1 else 20, "x", way)
+
+    def gather_far(way):
+        other = lax.rem(x - way + RING_X, RING_X)
+        piece = final_v.at[rep, final_rows(other), half_lanes(way)]
+        return copy_to(piece, piece, 21 if way == 1 else 22, "x", way)
 
     def share_rep():
-        return copy_to(final_v.at[rep], final_v.at[rep], 21, "rep", 0)
+        return copy_to(final_v.at[rep], final_v.at[rep], 23, "rep", 0)
 
     def landing(target, number, axis):
         return copy_to(target, target, number, axis, 1)
 
-    def weight_sums():
-        slope_ring.finish()
-        for part in range(RING_Y):
-            span = slice(part * HID_ROWS, (part + 1) * HID_ROWS)
-            one = jnp.zeros((FEAT_ROWS, HID_ROWS), F32)
-            two = jnp.zeros((FEAT_ROWS, HID_ROWS), F32)
-            for q in range(RING_Y):
-                piece = slope_all[q, :, span]
-                one = one + dot_plain(feat_own[:, q * CHUNK_COLS:(q + 1) * CHUNK_COLS], piece)
-                two = two + dot_plain(neigh_own[q], piece)
-            grad_v[0, :, span] = one
-            grad_v[1, :, span] = two
-            half_v[0, :, span] = one.astype(BF16)
-            half_v[1, :, span] = two.astype(BF16)
-        swap_rep().start()
-
-    def own_total():
+    def weight_sums(part):
+        span = slice(part * HID_ROWS, (part + 1) * HID_ROWS)
+        one = jnp.zeros((FEAT_ROWS, HID_ROWS), F32)
+        two = jnp.zeros((FEAT_ROWS, HID_ROWS), F32)
+        for q in range(RING_Y):
+            piece = slope_all[q, :, span]
+            one = one + dot_plain(feat_own[:, q * CHUNK_COLS:(q + 1) * CHUNK_COLS], piece)
+            two = two + dot_plain(jnp.concatenate([neigh_own[q, 0], neigh_own[q, 1]], axis=1), piece)
+        grad_v[0, :, span] = one
+        grad_v[1, :, span] = two
+        half_v[0, :, span] = one.astype(BF16)
+        half_v[1, :, span] = two.astype(BF16)
+        if part == RING_Y - 1:
+            swap_rep().start()
+
+    def own_total(q):
         weight = ws_full[feature_rows(me_y, 0, FEAT_ROWS), :]
-        for q in range(RING_Y):
-            span = slice(q * CHUNK_COLS, (q + 1) * CHUNK_COLS)
-            total_v[:, span] = total_v[:, span] + dot_rows(weight, slope_all[q])
+        span = slice(q * CHUNK_COLS, (q + 1) * CHUNK_COLS)
+        total_v[:, span] = total_v[:, span] + dot_rows(weight, slope_all[q])
 
     def hidden_leave():
         take_over(HIDDENS)
@@ -534,15 +550,24 @@
         landing(first_in, 0, "rep").wait_recv()
         sums[...] = grad_v[rep] + first_in[...].astype(F32)
         half_sums[...] = sums[...].astype(BF16)
-        for step in range(1, RING_X):
-            scatter_x(step).start()
+        for way in (1, -1):
+            relay_x(way).start()
+
+    def relayed_x():
+        for way in (1, -1):
+            number = 1 if way == 1 else 2
+            landing(relay_in.at[number - 1], number, "x").wait_recv()
+            rows_there = final_rows(lax.rem(x + way + RING_X, RING_X))
+            half_sums[rows_there, half_lanes(way)] = (
+                sums[rows_there, half_lanes(way)] + relay_in[number - 1].astype(F32)).astype(BF16)
+            scatter_x(way).start()
 
     def after_x():
-        for step in range(1, RING_X):
-            landing(second_in.at[step - 1], step, "x").wait_recv()
+        for number in (3, 4):
+            landing(second_in.at[number - 3], number, "x").wait_recv()
         mine = sums[pl.ds(pl.multiple_of(x * 48, 48), 48), :]
-        for step in range(1, RING_X):
-            mine = mine + second_in[step - 1].astype(F32)
+        for number in range(2):
+            mine = mine + second_in[number].astype(F32)
         for part in range(RING_Z):
             third_v[part] = mine[:, part * EDGE:(part + 1) * EDGE]
             third_half[part] = mine[:, part * EDGE:(part + 1) * EDGE].astype(BF16)
@@ -551,7 +576,7 @@
 
     def after_z():
         for step in range(1, RING_Z):
-            landing(third_in.at[step - 1], 3 + step, "z").wait_recv()
+            landing(third_in.at[step - 1], 4 + step, "z").wait_recv()
         value = third_v[z]
         for step in range(1, RING_Z):
             value = value + third_in[step - 1].astype(F32)
@@ -561,17 +586,27 @@
 
     def gathered_z():
         for step in range(1, RING_Z):
-            landing(final_v.at[rep, final_rows(x), final_lanes(lax.rem(z - step + RING_Z, RING_Z))], 10 + step, "z").wait_recv()
-        for step in range(1, RING_X):
-            gather_x(step).start()
+            landing(final_v.at[rep, final_rows(x), final_lanes(lax.rem(z - step + RING_Z, RING_Z))], 11 + step, "z").wait_recv()
+        for way in (1, -1):
+            gather_x(way).start()
+
+    def gathered_near():
+        for way in (1, -1):
+            other = lax.rem(x - way + RING_X, RING_X)
+            landing(final_v.at[rep, final_rows(other), :], 19 if way == 1 else 20, "x").wait_recv()
+            gather_far(way).start()
 
     def gathered_x():
-        for step in range(1, RING_X):
-            landing(final_v.at[rep, final_rows(lax.rem(x - step + RING_X, RING_X)), :], 17 + step, "x").wait_recv()
+        for way in (1, -1):
+            far = final_v.at[rep, final_rows(lax.rem(x + 2, RING_X)), half_lanes(way)]
+            landing(far, 21 if way == 1 else 22, "x").wait_recv()
         share_rep().start()
 
-    side = {6: slope_ring.hand_on, 14: weight_sums, 16: own_total, 20: after_rep, 30: hidden_leave, 34: after_x,
-            48: after_z, 61: gathered_z, 73: gathered_x}
+    side = {5: slope_ring.hand_on, 10: slope_ring.finish, 16: after_rep, 23: relayed_x, 25: hidden_leave, 33: after_x,
+            43: after_z, 53: gathered_z, 61: gathered_near, 69: gathered_x}
+    for part in range(RING_Y):
+        side[11 + part] = functools.partial(weight_sums, part)
+        side[35 + part] = functools.partial(own_total, part)
     arrived = 0
     for kind, i in back_steps:
         if kind == "recv":
@@ -585,7 +620,7 @@
         else:
             message(i).start()
 
-    landing(final_v.at[1 - rep], 21, "rep").wait_recv()
+    landing(final_v.at[1 - rep], 23, "rep").wait_recv()
     outputs = [pltpu.make_async_copy(final_v, sums_hbm, local_sem.at[18])]
     for copy in outputs:
         copy.start()
@@ -593,16 +628,18 @@
     outputs.append(pltpu.make_async_copy(grad_v16, grad_hbm, local_sem.at[16]))
     outputs[-1].start()
     swap_rep().wait_send()
-    for step in range(1, RING_X):
-        scatter_x(step).wait_send()
-        gather_x(step).wait_send()
+    for way in (1, -1):
+        relay_x(way).wait_send()
+        scatter_x(way).wait_send()
+        gather_x(way).wait_send()
+        gather_far(way).wait_send()
     for step in range(1, RING_Z):
         scatter_z(step).wait_send()
         gather_z(step).wait_send()
     share_rep().wait_send()
     for ring in (ws_ring, wn_ring, slope_ring):
         ring.drain()
-    for which in range(5):
+    for which in range(len(exchanges)):
         for step in range(1, RING_Y):
             hand_over(which, step).wait_send()
     hidden_out.wait()
@@ -673,8 +710,8 @@
             pltpu.VMEM((RING_Y, CHUNK_COLS, HID_ROWS), BF16),
             pltpu.VMEM((SHARD_COLS, HID_ROWS), BF16),
             pltpu.VMEM((CHUNK_COLS, SHARD_COLS), BF16),
-            pltpu.VMEM((RING_Y, FEAT_ROWS, CHUNK_COLS), BF16),
-            pltpu.VMEM((RING_Y * FEAT_ROWS, CHUNK_COLS), BF16),
+            pltpu.VMEM((RING_Y, 2, FEAT_ROWS, EDGE), BF16),
+            pltpu.VMEM((2, RING_Y * FEAT_ROWS, EDGE), BF16),
             pltpu.VMEM((RING_Y, CHUNK_COLS, SHARD_COLS), BF16),
             pltpu.VMEM((CHUNK_COLS, SHARD_COLS), F32),
             pltpu.VMEM((RING_Y, 2, FEAT_ROWS, EDGE), BF16),
@@ -688,7 +725,8 @@
             pltpu.VMEM((2, FEAT_ROWS, SHARD_COLS), BF16),
             pltpu.VMEM((FEAT_ROWS, SHARD_COLS), BF16),
             pltpu.VMEM((FEAT_ROWS, SHARD_COLS), BF16),
-            pltpu.VMEM((3, 48, SHARD_COLS), BF16),
+            pltpu.VMEM((2, 48, SHARD_COLS // 2), BF16),
+            pltpu.VMEM((2, 48, SHARD_COLS), BF16),
             pltpu.VMEM((7, 48, EDGE), BF16),
             pltpu.VMEM((8, 48, EDGE), F32),
             pltpu.VMEM((8, 48, EDGE), BF16),
@@ -698,8 +736,8 @@
             dma((len(found),)), dma((len(found),)),
             dma((len(found),)), dma((len(found),)),
             dma((12,)), dma((12,)),
-            dma((15,)), dma((15,)),
-            dma((22,)), dma((22,)),
+            dma((21,)), dma((21,)),
+            dma((24,)), dma((24,)),
             dma((19,)),
         ],
         compiler_params=pltpu.CompilerParams(

time: 181 us -> 178 us (0.983)
  Pallas kernels: 179 us -> 176 us
    pallas_call x1, Pallas kernels: 176 us -> 174 us  [shards(): pl.pallas_call(functools.partial(layer_kernel, found, steps, back_steps,...]
where the time goes in v5:
time: 178 us; the launch traced here: 177 us
  Pallas kernels  176 us (99%)
    pallas_call x1, Pallas kernels, shards(): pl.pallas_call(functools.partial(layer_kernel, found, steps, back_steps,...  174 us

profile of v5, /device:TPU:8, one launch (start us, length us, event | category | flops | bytes accessed | tf_op | source)
XLA Modules:
  0.0 177.1 jit_solution(11706481540157038045)
XLA Ops:
  0.6 173.8 %layer.1 = (bf16[1024,256]{1,0:T(8,128)(2,1)}, bf16[192,1024]{1,0:T(8,128)(2,1)}, bf16[2,192,1024]{2,1,0:T(8,128)(2,1)}) custom-call(bf16[192,1024]{1,0:T(8,128)(2,1)} %bitcast.15, s32[8,16]{1,0:T(8,128)} %bitcast.17, s32[8]{0:T(128)} %bitcast.19, bf16[128,128,128]{2,1,0:T(8,128)(2,1)} %bitcast.12, bf16[192,1024]{1,0:T(8,128)(2,1)} %ws_hbm.1, ...), custom_call_target="tpu_custom_call" | custom-call | flops 6000000000 | bytes 20000000 | tf_op jit(solution)/shard_map/layer/pallas_call | solution.py:696
  174.4 2.7 %finish.1 = (bf16[1024,256]{1,0:T(8,128)(2,1)}, bf16[192,1024]{1,0:T(8,128)(2,1)}, f32[192,1024]{1,0:T(8,128)}, f32[192,1024]{1,0:T(8,128)}) custom-call(bf16[1024,256]{1,0:T(8,128)(2,1)} %get-tuple-element.11.hidden_in, bf16[192,1024]{1,0:T(8,128)(2,1)} %get-tuple-element.12.grad_in, bf16[2,192,1024]{2,1,0:T(8,128)(2,1)} %get-tuple-element.13.sums_in), custom_call_target="tpu_custom_call" | custom-call | tf_op jit(solution)/shard_map/finish/pallas_call | solution.py:747

commit v6 on v5

--- a/solution.py
+++ b/solution.py
@@ -23,7 +23,7 @@
 CHUNK_COLS = SHARD_COLS // CHUNKS
 SPLIT_A = 80
 LIMIT = 3
-DELAY = 30.0
+DELAY = 40.0
 
 
 class Message:
@@ -412,8 +412,8 @@
     seg[128] = jnp.zeros((FEAT_ROWS, EDGE), BF16)
 
     def spread(turn, carry):
-        for inner in range(8):
-            p = turn * 8 + inner
+        for inner in range(32):
+            p = turn * 32 + inner
             slot = plan[1, p]
             part = dot_plain(back_v[plan[2, p]], tiles_v[slot])
             keep = plan[3, p].astype(F32)
@@ -423,7 +423,7 @@
         return carry
 
     total_v[:, 0:EDGE] = jnp.zeros((FEAT_ROWS, EDGE), F32)
-    lax.fori_loop(0, 16, spread, 0)
+    lax.fori_loop(0, 4, spread, 0)
 
     def fill(owner, carry):
         for part in range(8):

time: 178 us -> 178 us (level)
  no operation moved by 1% of the time
where the time goes in v6:
time: 178 us; the launch traced here: 177 us
  Pallas kernels  176 us (99%)
    pallas_call x1, Pallas kernels, shards(): pl.pallas_call(functools.partial(layer_kernel, found, steps, back_steps,...  173 us

profile of v6, /device:TPU:8, one launch (start us, length us, event | category | flops | bytes accessed | tf_op | source)
XLA Modules:
  0.0 176.6 jit_solution(9600354267216069146)
XLA Ops:
  0.6 173.3 %layer.1 = (bf16[1024,256]{1,0:T(8,128)(2,1)}, bf16[192,1024]{1,0:T(8,128)(2,1)}, bf16[2,192,1024]{2,1,0:T(8,128)(2,1)}) custom-call(bf16[192,1024]{1,0:T(8,128)(2,1)} %bitcast.15, s32[8,16]{1,0:T(8,128)} %bitcast.17, s32[8]{0:T(128)} %bitcast.19, bf16[128,128,128]{2,1,0:T(8,128)(2,1)} %bitcast.12, bf16[192,1024]{1,0:T(8,128)(2,1)} %ws_hbm.1, ...), custom_call_target="tpu_custom_call" | custom-call | flops 6000000000 | bytes 20000000 | tf_op jit(solution)/shard_map/layer/pallas_call | solution.py:696
  173.9 2.7 %finish.1 = (bf16[1024,256]{1,0:T(8,128)(2,1)}, bf16[192,1024]{1,0:T(8,128)(2,1)}, f32[192,1024]{1,0:T(8,128)}, f32[192,1024]{1,0:T(8,128)}) custom-call(bf16[1024,256]{1,0:T(8,128)(2,1)} %get-tuple-element.11.hidden_in, bf16[192,1024]{1,0:T(8,128)(2,1)} %get-tuple-element.12.grad_in, bf16[2,192,1024]{2,1,0:T(8,128)(2,1)} %get-tuple-element.13.sums_in), custom_call_target="tpu_custom_call" | custom-call | tf_op jit(solution)/shard_map/finish/pallas_call | solution.py:747

commit v7 on v6

--- a/solution.py
+++ b/solution.py
@@ -454,14 +454,17 @@
         def rows(step, carry):
             here = pl.ds(pl.multiple_of(offsets[i] + step * 16, 16), 16)
             there = pl.ds(pl.multiple_of(m.low + step * 16, 16), 16)
-            for part in range(8):
-                value = landed[part, here, :].astype(F32)
-                if mine:
-                    span = slice(part * EDGE, (part + 1) * EDGE)
-                    total_v[there, span] = total_v[there, span] + value
-                else:
-                    place = owner * 8 + part
-                    table[place, there, :] = (table[place, there, :].astype(F32) + value).astype(BF16)
+            values = [landed[part, here, :].astype(F32) for part in range(8)]
+            if mine:
+                spans = [slice(part * EDGE, (part + 1) * EDGE) for part in range(8)]
+                values = [total_v[there, span] + value for span, value in zip(spans, values)]
+                for span, value in zip(spans, values):
+                    total_v[there, span] = value
+            else:
+                values = [(table[owner * 8 + part, there, :].astype(F32) + value).astype(BF16)
+                          for part, value in enumerate(values)]
+                for part, value in enumerate(values):
+                    table[owner * 8 + part, there, :] = value
             return carry
 
         lax.fori_loop(0, m.size // 16, rows, 0)

time: 178 us -> 178 us (level)
  no operation moved by 1% of the time
where the time goes in v7:
time: 178 us; the launch traced here: 177 us
  Pallas kernels  176 us (99%)
    pallas_call x1, Pallas kernels, shards(): pl.pallas_call(functools.partial(layer_kernel, found, steps, back_steps,...  173 us

profile of v7, /device:TPU:8, one launch (start us, length us, event | category | flops | bytes accessed | tf_op | source)
XLA Modules:
  0.0 176.6 jit_solution(9600354267216069146)
XLA Ops:
  0.6 173.3 %layer.1 = (bf16[1024,256]{1,0:T(8,128)(2,1)}, bf16[192,1024]{1,0:T(8,128)(2,1)}, bf16[2,192,1024]{2,1,0:T(8,128)(2,1)}) custom-call(bf16[192,1024]{1,0:T(8,128)(2,1)} %bitcast.15, s32[8,16]{1,0:T(8,128)} %bitcast.17, s32[8]{0:T(128)} %bitcast.19, bf16[128,128,128]{2,1,0:T(8,128)(2,1)} %bitcast.12, bf16[192,1024]{1,0:T(8,128)(2,1)} %ws_hbm.1, ...), custom_call_target="tpu_custom_call" | custom-call | flops 6000000000 | bytes 20000000 | tf_op jit(solution)/shard_map/layer/pallas_call | solution.py:699
  173.9 2.7 %finish.1 = (bf16[1024,256]{1,0:T(8,128)(2,1)}, bf16[192,1024]{1,0:T(8,128)(2,1)}, f32[192,1024]{1,0:T(8,128)}, f32[192,1024]{1,0:T(8,128)}) custom-call(bf16[1024,256]{1,0:T(8,128)(2,1)} %get-tuple-element.11.hidden_in, bf16[192,1024]{1,0:T(8,128)(2,1)} %get-tuple-element.12.grad_in, bf16[2,192,1024]{2,1,0:T(8,128)(2,1)} %get-tuple-element.13.sums_in), custom_call_target="tpu_custom_call" | custom-call | tf_op jit(solution)/shard_map/finish/pallas_call | solution.py:750

commit v8 on v7

--- a/solution.py
+++ b/solution.py
@@ -412,8 +412,8 @@
     seg[128] = jnp.zeros((FEAT_ROWS, EDGE), BF16)
 
     def spread(turn, carry):
-        for inner in range(32):
-            p = turn * 32 + inner
+        for inner in range(64):
+            p = turn * 64 + inner
             slot = plan[1, p]
             part = dot_plain(back_v[plan[2, p]], tiles_v[slot])
             keep = plan[3, p].astype(F32)
@@ -423,7 +423,7 @@
         return carry
 
     total_v[:, 0:EDGE] = jnp.zeros((FEAT_ROWS, EDGE), F32)
-    lax.fori_loop(0, 4, spread, 0)
+    lax.fori_loop(0, 2, spread, 0)
 
     def fill(owner, carry):
         for part in range(8):

time: 178 us -> 178 us (level)
  no operation moved by 1% of the time
where the time goes in v8:
time: 178 us; the launch traced here: 177 us
  Pallas kernels  176 us (99%)
    pallas_call x1, Pallas kernels, shards(): pl.pallas_call(functools.partial(layer_kernel, found, steps, back_steps,...  173 us

profile of v8, /device:TPU:8, one launch (start us, length us, event | category | flops | bytes accessed | tf_op | source)
XLA Modules:
  0.0 176.8 jit_solution(4889377895662808921)
XLA Ops:
  0.6 173.3 %layer.1 = (bf16[1024,256]{1,0:T(8,128)(2,1)}, bf16[192,1024]{1,0:T(8,128)(2,1)}, bf16[2,192,1024]{2,1,0:T(8,128)(2,1)}) custom-call(bf16[192,1024]{1,0:T(8,128)(2,1)} %bitcast.15, s32[8,16]{1,0:T(8,128)} %bitcast.17, s32[8]{0:T(128)} %bitcast.19, bf16[128,128,128]{2,1,0:T(8,128)(2,1)} %bitcast.12, bf16[192,1024]{1,0:T(8,128)(2,1)} %ws_hbm.1, ...), custom_call_target="tpu_custom_call" | custom-call | flops 6000000000 | bytes 20000000 | tf_op jit(solution)/shard_map/layer/pallas_call | solution.py:699
  173.9 2.7 %finish.1 = (bf16[1024,256]{1,0:T(8,128)(2,1)}, bf16[192,1024]{1,0:T(8,128)(2,1)}, f32[192,1024]{1,0:T(8,128)}, f32[192,1024]{1,0:T(8,128)}) custom-call(bf16[1024,256]{1,0:T(8,128)(2,1)} %get-tuple-element.11.hidden_in, bf16[192,1024]{1,0:T(8,128)(2,1)} %get-tuple-element.12.grad_in, bf16[2,192,1024]{2,1,0:T(8,128)(2,1)} %get-tuple-element.13.sums_in), custom_call_target="tpu_custom_call" | custom-call | tf_op jit(solution)/shard_map/finish/pallas_call | solution.py:750
